TPU v7x, 32 devices: a whole 2x2x4 slice. The times are simulated.
32 devices in a mesh: ctx: 4 (over y, x), exp: 8 (over z, core).
Axes of the slice: x: 2, y: 2, z: 4, core: 2. Of those that a mesh axis runs over, the one named last changes fastest.
Arguments:
- query: bfloat16 [8, 512, 2048], P('exp', 'ctx'), may hold values from -8 to 8
- key_value: bfloat16 [8, 512, 256], P('exp', 'ctx'), may hold values from -8 to 8
- prior_out: bfloat16 [8, 512, 2048], P('exp', 'ctx'), may hold values from -6 to 6
- prior_lse: float32 [8, 512, 32], P('exp', 'ctx'), may hold values from 5 to 9
- norm_gain: float32 [2048], replicated, may hold values from 0.25 to 1.75
- w_gate: bfloat16 [8, 2048, 768], P('exp'), may hold values from -0.125 to 0.125
- w_up: bfloat16 [8, 2048, 768], P('exp'), may hold values from -0.125 to 0.125
- expert_ids: int32 [8, 512, 2], P('exp', 'ctx'), may hold values from 0 to 7, all different within a row; in each aligned block of 128 rows (0 to 127, 128 to 255, ..., all dimensions but the last counted through in order) at most 48 rows name the same one
- route_weight: bfloat16 [8, 512, 2], P('exp', 'ctx'), may hold values from 0.099609375 to 1
Outputs:
- attended: bfloat16 [8, 512, 2048], P('exp', 'ctx')
- expert_hidden: bfloat16 [4, 8, 384, 768], P('ctx', 'exp')
Inputs may be any that keep to these rules, and one draw needn't show every extreme that they name: `expert_ids`: each token names 2 different experts; the rows of one device name one expert at most 48 times, a bound that some block reaches.
All inputs are finite; a program needn't handle non-finite values.
Results may differ from a plain program's by a relative error of at most 0.0072.
Values may be sent and summed in bfloat16 or wider, within the bound.
A program may use at most 64 MiB of HBM per device.

v0:
```python
import jax
import jax.numpy as jnp
from jax import lax
from jax.sharding import PartitionSpec as P

HQ = 32
KVH = 2
HD = 64
FF = 768
STEPS = 3
IN_FLIGHT = 2


def passed_along(block, axis, distance):
    devices = range(lax.axis_size(axis))
    route = [((i - distance) % len(devices), i) for i in devices]
    return lax.ppermute(block, axis, route)


def folded_positions(block_index, row_count, block_total):
    offset = jnp.arange(row_count, dtype=jnp.int32)
    half_rows = row_count // 2
    return jnp.where(
        offset < half_rows,
        block_index * half_rows + offset,
        (2 * block_total - 1 - block_index) * half_rows + offset - half_rows,
    )


def attend_local(queries, window, window_pos, query_pos, prior_rows, prior_logs):
    row_count = queries.shape[0]
    key_count = window.shape[0]
    group_size = HQ // KVH
    grouped = jnp.transpose(queries.reshape(row_count, KVH, group_size, HD), (1, 0, 2, 3))
    grouped = grouped.reshape(KVH, row_count * group_size, HD)
    key_rows = jnp.transpose(window[:, : KVH * HD].reshape(key_count, KVH, HD), (1, 0, 2))
    value_rows = jnp.transpose(window[:, KVH * HD :].reshape(key_count, KVH, HD), (1, 0, 2))
    scores = jnp.einsum(
        "gqd,gsd->gqs", grouped, key_rows, preferred_element_type=jnp.float32
    ) * HD ** (-0.5)
    scores = scores.reshape(KVH, row_count, group_size, key_count)
    allowed = (window_pos[None, :] <= query_pos[:, None])[None, :, None, :]
    scores = jnp.where(allowed, scores, -1e30)
    logs = jnp.transpose(prior_logs.reshape(row_count, KVH, group_size), (1, 0, 2))
    row_max = jnp.maximum(jnp.max(scores, axis=-1), logs)
    powers = jnp.exp(scores - row_max[..., None])
    carried = jnp.exp(logs - row_max)
    denominator = carried + jnp.sum(powers, axis=-1)
    powers_low = powers.astype(jnp.bfloat16).reshape(KVH, row_count * group_size, key_count)
    mixed = jnp.einsum("gqs,gsd->gqd", powers_low, value_rows, preferred_element_type=jnp.float32)
    mixed = mixed.reshape(KVH, row_count, group_size, HD)
    earlier = jnp.transpose(
        prior_rows.reshape(row_count, KVH, group_size, HD), (1, 0, 2, 3)
    ).astype(jnp.float32)
    result = (carried[..., None] * earlier + mixed) / denominator[..., None]
    result = jnp.transpose(result, (1, 0, 2, 3))
    return result.reshape(row_count, HQ * HD).astype(jnp.bfloat16)


def normalize(row_block, gain_row):
    values = row_block.astype(jnp.float32)
    inverse = lax.rsqrt(jnp.mean(values * values, axis=-1, keepdims=True) + 1e-06)
    return (values * inverse * gain_row).astype(jnp.bfloat16)


def slot_sources(ids_flat, expert_total, capacity):
    assign_total = ids_flat.shape[0]
    onehot = (ids_flat[:, None] == jnp.arange(expert_total, dtype=jnp.int32)[None, :]).astype(
        jnp.int32
    )
    before = jnp.cumsum(onehot, axis=0) - onehot
    rank = jnp.sum(before * onehot, axis=1)
    slot_of = ids_flat * capacity + rank
    match = slot_of[None, :] == jnp.arange(expert_total * capacity, dtype=jnp.int32)[:, None]
    numbered = jnp.arange(assign_total, dtype=jnp.int32)[None, :] + 1
    return jnp.sum(jnp.where(match, numbered, 0), axis=1) - 1


def per_device(
    query, key_value, prior_out, prior_lse, norm_gain, w_gate, w_up, expert_ids, route_weight
):
    ctx_total = lax.axis_size("ctx")
    exp_total = lax.axis_size("exp")
    ctx_index = lax.axis_index("ctx")
    row_count = query.shape[1]
    own_pairs = key_value[0]
    blocks = [own_pairs]
    moving = own_pairs
    for step_index in range(1, STEPS):
        moving = passed_along(moving, "ctx", 1)
        blocks.append(moving)
    window = jnp.concatenate(blocks, axis=0)
    sources = (ctx_index - jnp.arange(STEPS, dtype=jnp.int32)) % ctx_total

    def block_positions(block_index):
        return folded_positions(block_index, row_count, ctx_total)

    window_pos = jax.vmap(block_positions)(sources).reshape(-1)
    query_pos = block_positions(ctx_index)
    attended = attend_local(query[0], window, window_pos, query_pos, prior_out[0], prior_lse[0])
    capacity = max(2, IN_FLIGHT * row_count * 3 // (2 * exp_total))
    source_of = slot_sources(expert_ids[0].reshape(-1), exp_total, capacity)
    filled = source_of >= 0
    clamped = jnp.maximum(source_of, 0)
    payload = jnp.where(
        filled[:, None], attended[clamped // IN_FLIGHT], jnp.zeros((), jnp.bfloat16)
    )
    payload = payload.reshape(exp_total, capacity, HQ * HD)
    slot_weights = jnp.where(
        filled, route_weight[0].reshape(-1)[clamped], jnp.zeros((), jnp.bfloat16)
    )
    slot_weights = slot_weights.reshape(exp_total, capacity)
    arrived_rows, arrived_weights = (
        lax.all_to_all(payload, "exp", split_axis=0, concat_axis=0, tiled=True),
        lax.all_to_all(slot_weights, "exp", split_axis=0, concat_axis=0, tiled=True),
    )
    row_block = arrived_rows
    row_block = normalize(row_block, norm_gain)
    flat_rows = row_block.reshape(-1, row_block.shape[-1])
    gate_out = jnp.dot(flat_rows, w_gate[0], preferred_element_type=jnp.float32)
    up_out = jnp.dot(flat_rows, w_up[0], preferred_element_type=jnp.float32)
    hidden = (
        jax.nn.silu(gate_out) * up_out * arrived_weights.astype(jnp.float32).reshape(-1)[:, None]
    )
    hidden = hidden.astype(jnp.bfloat16).reshape(row_block.shape[0], row_block.shape[1], FF)
    return (attended[None], hidden.reshape(1, 1, exp_total * capacity, FF))


def solution(mesh):
    placed = (
        P("exp", "ctx", None),
        P("exp", "ctx", None),
        P("exp", "ctx", None),
        P("exp", "ctx", None),
        P(),
        P("exp", None, None),
        P("exp", None, None),
        P("exp", "ctx", None),
        P("exp", "ctx", None),
    )
    return jax.shard_map(
        per_device,
        mesh=mesh,
        in_specs=placed,
        out_specs=(P("exp", "ctx", None), P("ctx", "exp", None, None)),
        check_vma=False,
    )
```

profile of v0, /device:TPU:0, one launch (start us, length us, event | category | flops | bytes accessed | tf_op | source)
XLA Modules:
  0.0 116.5 jit_solution(14212556855712981190)
XLA Ops:
  0.6 3.0 %collective-permute-start = (bf16[128,256]{1,0:T(8,128)(2,1)}, bf16[128,256]{1,0:T(8,128)(2,1)S(1)}, u32[]{:S(2)}, u32[]{:S(2)}) collective-permute-start(bf16[128,256]{1,0:T(8,128)(2,1)} %bitcast.89), channel_id=1, source_target_pairs={{24,0},{0,8},{8,16},{16,24},{25,1},{1,9},{9,17},{17,25},{26,2},{2,... | collective-permute-start | bytes 196616 | tf_op jit(solution)/shard_map/ppermute | solution.py:17
  3.6 0.8 copy.88
  4.7 0.6 reduce-window.6
  5.3 0.2 slice_reduce_fusion
  5.7 0.1 select_reduce_fusion
  5.8 0.8 copy.91
  6.8 2.7 %gather_fusion.1 = bf16[384]{0:T(512)(128)(2,1)S(1)} fusion(bf16[256]{0:T(256)(128)(2,1)S(1)} %reshape_squeeze.16, s32[1024]{0:T(1024)S(1)} %pad_clamp_fusion), kind=kCustom, calls=%fused_computation.1 | custom fusion | bytes 3072 | tf_op jit(solution)/shard_map/gather | solution.py:110
  9.5 0.7 select_n.98
  10.2 4.9 %all-to-all-start.1 = ((bf16[8,1,48]{2,1,0:T(2,128)(2,1)}), bf16[8,1,48]{2,1,0:T(2,128)(2,1)S(1)}, u32[]{:S(2)}, u32[]{:S(2)}) async-start(bf16[8,1,48]{2,1,0:T(2,128)(2,1)} %select_n.98), calls=%async_computation.1 | async-start | bytes 8192 | tf_op jit(solution)/shard_map/all_to_all | solution.py:115
  15.3 1.1 broadcast_in_dim.68
  16.4 2.8 %copy.75 = pred[2048,384]{0,1:T(8,128)(4,1)} copy(pred[2048,384]{1,0:T(8,128)(4,1)} %bitcast.79) | data formatting | bytes 1572864 | tf_op jit(solution)/shard_map/jit(_where)/broadcast_in_dim | solution.py:43
  19.2 2.0 %copy.77 = bf16[1,128,2048]{1,2,0:T(8,128)(2,1)} copy(bf16[1,128,2048]{2,1,0:T(8,128)(2,1)} %param.9) | data formatting | bytes 1048576 | tf_op args[0]
  21.2 2.8 %copy.78 = bf16[2,128,16,64]{3,2,1,0:T(8,128)(2,1)} copy(bf16[2,128,16,64]{1,3,2,0:T(8,128)(2,1)} %bitcast.80) | data formatting | bytes 1048576 | tf_op jit(solution)/shard_map/transpose | solution.py:34
  24.0 2.0 %copy.81 = bf16[1,128,2048]{1,2,0:T(8,128)(2,1)} copy(bf16[1,128,2048]{2,1,0:T(8,128)(2,1)} %param.11) | data formatting | bytes 1048576 | tf_op args[2]
  26.1 1.7 %collective-permute-start.1 = (bf16[128,256]{1,0:T(8,128)(2,1)S(1)}, bf16[128,256]{1,0:T(8,128)(2,1)S(1)}, u32[]{:S(2)}, u32[]{:S(2)}) collective-permute-start(bf16[128,256]{1,0:T(8,128)(2,1)S(1)} %collective-permute-done), channel_id=1, source_target_pairs={{24,0},{0,8},{8,16},{16,24},{25,1},{1,9},{9,17},{17,25},{26,2},{2,... | collective-permute-start | bytes 196616 | tf_op jit(solution)/shard_map/ppermute | solution.py:17
  27.9 3.9 %collective-permute-done.1 = bf16[128,256]{1,0:T(8,128)(2,1)S(1)} collective-permute-done((bf16[128,256]{1,0:T(8,128)(2,1)S(1)}, bf16[128,256]{1,0:T(8,128)(2,1)S(1)}, u32[]{:S(2)}, u32[]{:S(2)}) %collective-permute-start.1) | collective-permute-done | bytes 65568 | tf_op jit(solution)/shard_map/ppermute | solution.py:17
  31.9 5.5 %fusion.2 = (f32[2,2048]{1,0:T(2,128)S(1)}, f32[2,384,2048]{2,1,0:T(8,128)}) fusion(pred[2048,384]{0,1:T(8,128)(4,1)} %copy.75, bf16[2,384,64]{1,2,0:T(8,128)(2,1)S(1)} %bitcast.85, bf16[2,2048,64]{2,1,0:T(8,128)(2,1)} %bitcast.78), kind=kOutput, calls=%fused_computation.6 | convolution fusion | flops 206041088 | bytes 7716864 | tf_op jit(solution)/shard_map/gqd,gsd->gqs/dot_general | solution.py:38
  37.9 4.4 %fusion = f32[2,2048]{1,0:T(2,128)S(1)} fusion(f32[2,384,2048]{2,1,0:T(8,128)} %get-tuple-element.19, f32[2,2048]{1,0:T(2,128)S(1)} %sub.65, pred[2048,384]{0,1:T(8,128)(4,1)} %copy.75), kind=kLoop, calls=%fused_computation.4 | loop fusion | flops 6287360 | bytes 7110656 | tf_op jit(solution)/shard_map/reduce_sum | solution.py:48
  42.6 6.4 %fusion.6 = f32[2,2048,64]{2,1,0:T(8,128)} fusion(bf16[2,384,64]{1,2,0:T(8,128)(2,1)S(1)} %bitcast.86, f32[2,384,2048]{2,1,0:T(8,128)} %get-tuple-element.19, f32[2,2048]{1,0:T(2,128)S(1)} %sub.65, pred[2048,384]{0,1:T(8,128)(4,1)} %copy.75), kind=kOutput, calls=%fused_computation.12 | convolution fusion | flops 207618048 | bytes 8241152 | tf_op jit(solution)/shard_map/gqs,gsd->gqd/dot_general | solution.py:50
  49.0 3.3 %copy.86 = f32[2,128,16,64]{1,3,2,0:T(8,128)} copy(f32[2,128,16,64]{3,2,1,0:T(8,128)} %bitcast.81) | data formatting | bytes 2097152 | tf_op jit(solution)/shard_map/reshape | solution.py:51
  52.3 2.4 %fusion.31 = bf16[2,128,16,64]{1,3,2,0:T(8,128)(2,1)} fusion(f32[2,128,16,64]{1,3,2,0:T(8,128)} %copy.86, bf16[128,2,16,64]{0,3,2,1:T(8,128)(2,1)} %bitcast.82, f32[2,128,16]{1,2,0:T(8,128)S(1)} %get-tuple-element.12, f32[2,128,16]{1,2,0:T(8,128)S(1)} %get-tuple-element.13), kind=kLoop, calls=%fused_computation.30 | loop fusion | flops 1310720 | bytes 2129920 | tf_op jit(solution)/shard_map/convert_element_type | solution.py:57
  54.7 2.0 %copy.90 = bf16[128,2048]{1,0:T(8,128)(2,1)} copy(bf16[128,2048]{0,1:T(8,128)(2,1)} %bitcast.76) | data formatting | bytes 1048576 | tf_op jit(solution)/shard_map/convert_element_type | solution.py:57
  56.8 6.2 %gather_fusion = bf16[384,2048]{1,0:T(8,128)(2,1)} fusion(bf16[128,2048]{1,0:T(8,128)(2,1)} %copy.90, s32[1024]{0:T(1024)S(1)} %pad_clamp_fusion.1), kind=kCustom, calls=%fused_computation | custom fusion | bytes 3147264 | tf_op jit(solution)/shard_map/gather | solution.py:106
  63.0 2.7 %broadcast_select_fusion = bf16[8,48,2048]{2,1,0:T(8,128)(2,1)} fusion(bf16[8,48,2048]{2,1,0:T(8,128)(2,1)} %bitcast.75, pred[8,48]{1,0:T(8,128)(4,1)S(1)} %ge.20), kind=kLoop, calls=%fused_computation.21 | loop fusion | flops 786432 | bytes 3146112 | tf_op jit(solution)/shard_map/jit(_where)/select_n | solution.py:105
  65.7 5.0 %all-to-all-start = ((bf16[8,48,2048]{2,1,0:T(8,128)(2,1)}), bf16[8,48,2048]{2,1,0:T(8,128)(2,1)}, u32[]{:S(2)}, u32[]{:S(2)}) async-start(bf16[8,48,2048]{2,1,0:T(8,128)(2,1)} %broadcast_select_fusion), calls=%async_computation | async-start | bytes 3145728 | tf_op jit(solution)/shard_map/all_to_all | solution.py:114
  70.8 2.0 %copy.93 = bf16[1,128,2048]{2,1,0:T(8,128)(2,1)} copy(bf16[1,128,2048]{1,2,0:T(8,128)(2,1)} %bitcast.77) | data formatting | bytes 1048576
  72.8 35.8 %all-to-all-done = bf16[8,48,2048]{2,1,0:T(8,128)(2,1)} async-done(((bf16[8,48,2048]{2,1,0:T(8,128)(2,1)}), bf16[8,48,2048]{2,1,0:T(8,128)(2,1)}, u32[]{:S(2)}, u32[]{:S(2)}) %all-to-all-start) | async-done | bytes 1572896 | tf_op jit(solution)/shard_map/all_to_all | solution.py:114
  108.6 1.8 %fusion.3 = f32[8,48]{1,0:T(8,128)S(1)} fusion(bf16[8,48,2048]{2,1,0:T(8,128)(2,1)} %all-to-all-done), kind=kLoop, calls=%fused_computation.9 | loop fusion | flops 2358912 | bytes 1574400 | tf_op jit(solution)/shard_map/reduce_sum | solution.py:62
  110.4 1.8 %fusion.5 = bf16[8,48,2048]{2,1,0:T(8,128)(2,1)S(1)} fusion(bf16[8,48,2048]{2,1,0:T(8,128)(2,1)} %all-to-all-done, f32[2048]{0:T(1024)S(1)} %copy-done.3, f32[8,48]{1,0:T(8,128)S(1)} %add_rsqrt_fusion), kind=kLoop, calls=%fused_computation.11 | loop fusion | flops 3145728 | bytes 3155456 | tf_op jit(solution)/shard_map/convert_element_type | solution.py:63
  112.3 1.4 %fusion.10 = f32[384,768]{1,0:T(8,128)S(1)} fusion(bf16[384,2048]{1,0:T(8,128)(2,1)S(1)} %bitcast.83, bf16[1,2048,768]{2,1,0:T(8,128)(2,1)S(1)} %copy-done), kind=kOutput, calls=%fused_computation.15 | convolution fusion | flops 1207959552 | bytes 5898240 | tf_op jit(solution)/shard_map/dot_general | solution.py:120
  113.7 0.5 copy-done.4
  114.2 2.3 %fusion.25 = bf16[1,1,384,768]{3,2,1,0:T(8,128)(2,1)} fusion(bf16[384,2048]{1,0:T(8,128)(2,1)S(1)} %bitcast.84, bf16[1,2048,768]{2,1,0:T(8,128)(2,1)S(1)} %copy-done.4, f32[384,768]{1,0:T(8,128)S(1)} %fusion.10, f32[384]{0:T(512)S(1)} %reshape.296), kind=kOutput, calls=%fused_computation.25 | convolution fusion | flops 1210023936 | bytes 6489600 | tf_op jit(solution)/shard_map/dot_general | solution.py:121
  (46 shorter events, 1.9 us)
Async XLA Ops:
  0.6 111.7 %copy-start = (bf16[1,2048,768]{2,1,0:T(8,128)(2,1)S(1)}, bf16[1,2048,768]{2,1,0:T(8,128)(2,1)}, u32[]{:S(2)}) copy-start(bf16[1,2048,768]{2,1,0:T(8,128)(2,1)} %param.14) | copy-start | bytes 9437188
  0.6 25.5 %collective-permute-start = (bf16[128,256]{1,0:T(8,128)(2,1)}, bf16[128,256]{1,0:T(8,128)(2,1)S(1)}, u32[]{:S(2)}, u32[]{:S(2)}) collective-permute-start(bf16[128,256]{1,0:T(8,128)(2,1)} %bitcast.89), channel_id=1, source_target_pairs={{24,0},{0,8},{8,16},{16,24},{25,1},{1,9},{9,17},{17,25},{26,2},{2,... | collective-permute-start | bytes 196616 | tf_op jit(solution)/shard_map/ppermute | solution.py:17
  9.5 22.3 %copy-start.2 = (bf16[1,128,256]{2,1,0:T(8,128)(2,1)S(1)}, bf16[1,128,256]{2,1,0:T(8,128)(2,1)}, u32[]{:S(2)}) copy-start(bf16[1,128,256]{2,1,0:T(8,128)(2,1)} %param.10) | copy-start | bytes 196612
  10.2 55.5 %all-to-all-start.1 = ((bf16[8,1,48]{2,1,0:T(2,128)(2,1)}), bf16[8,1,48]{2,1,0:T(2,128)(2,1)S(1)}, u32[]{:S(2)}, u32[]{:S(2)}) async-start(bf16[8,1,48]{2,1,0:T(2,128)(2,1)} %select_n.98), calls=%async_computation.1 | async-start | bytes 8192 | tf_op jit(solution)/shard_map/all_to_all | solution.py:115
  26.1 5.6 %collective-permute-start.1 = (bf16[128,256]{1,0:T(8,128)(2,1)S(1)}, bf16[128,256]{1,0:T(8,128)(2,1)S(1)}, u32[]{:S(2)}, u32[]{:S(2)}) collective-permute-start(bf16[128,256]{1,0:T(8,128)(2,1)S(1)} %collective-permute-done), channel_id=1, source_target_pairs={{24,0},{0,8},{8,16},{16,24},{25,1},{1,9},{9,17},{17,25},{26,2},{2,... | collective-permute-start | bytes 196616 | tf_op jit(solution)/shard_map/ppermute | solution.py:17
  31.9 5.7 %copy-start.1 = (f32[1,128,32]{1,2,0:T(8,128)S(1)}, f32[1,128,32]{1,2,0:T(8,128)}, u32[]{:S(2)}) copy-start(f32[1,128,32]{1,2,0:T(8,128)} %param.12) | copy-start | bytes 49156
  65.7 44.7 %copy-start.3 = (f32[2048]{0:T(1024)S(1)}, f32[2048]{0:T(1024)}, u32[]{:S(2)}) copy-start(f32[2048]{0:T(1024)} %param.13) | copy-start | bytes 24580
  65.7 42.9 %all-to-all-start = ((bf16[8,48,2048]{2,1,0:T(8,128)(2,1)}), bf16[8,48,2048]{2,1,0:T(8,128)(2,1)}, u32[]{:S(2)}, u32[]{:S(2)}) async-start(bf16[8,48,2048]{2,1,0:T(8,128)(2,1)} %broadcast_select_fusion), calls=%async_computation | async-start | bytes 3145728 | tf_op jit(solution)/shard_map/all_to_all | solution.py:114
  112.3 1.9 %copy-start.4 = (bf16[1,2048,768]{2,1,0:T(8,128)(2,1)S(1)}, bf16[1,2048,768]{2,1,0:T(8,128)(2,1)}, u32[]{:S(2)}) copy-start(bf16[1,2048,768]{2,1,0:T(8,128)(2,1)} %param.15) | copy-start | bytes 9437188
where the time goes:
time: 117 us; the launch traced here: 116 us
  waiting for transfers between devices  39.7 us (34%)
  local copies, waits for them, and re-layouts  31.3 us (27%)
  matrix products  15.7 us (13%)
  starting transfers between devices  14.6 us (12%)
  other arithmetic  14.4 us (12%)
    all_to_all x1, waiting for transfers between devices, per_device(): lax.all_to_all(payload, 'exp', split_axis=0, concat_axis=0, tiled=True)  35.8 us
    unnamed x15, local copies, waits for them, and re-layouts  8.18 us
    dot_general x1, matrix products, attend_local(): jnp.einsum('gqs,gsd->gqd', powers_low, value_rows, preferred_element_type...  6.44 us
    gather x1, local copies, waits for them, and re-layouts, per_device(): attended[clamped // IN_FLIGHT]  6.18 us
    dot_general x1, matrix products, attend_local(): jnp.einsum('gqd,gsd->gqs', grouped, key_rows, preferred_element_type=jnp....  5.51 us
    all_to_all x1, starting transfers between devices, per_device(): lax.all_to_all(payload, 'exp', split_axis=0, concat_axis=0, tiled=True)  4.99 us
    all_to_all x1, starting transfers between devices, per_device(): lax.all_to_all(slot_weights, 'exp', split_axis=0, concat_axis=0, tiled=True)  4.88 us
    ppermute x2, starting transfers between devices, passed_along(): return lax.ppermute(block, axis, route)  4.71 us
  transfers between devices with their start and end apart: 4, of which 2 were waited for; matrix products, arithmetic and copies ran while one was open for 46% of the time, Pallas kernels for 0%

commit v1 on v0

v1 whole, which is shorter than its diff:
```python
import functools

import jax
import jax.numpy as jnp
from jax import lax
from jax.experimental import pallas as pl
from jax.experimental.pallas import tpu as pltpu
from jax.sharding import PartitionSpec as P

HQ = 32
KVH = 2
HD = 64
FF = 768
STEPS = 3
IN_FLIGHT = 2

MESH = pl.DeviceIdType.MESH
WIDE = 256
QUAD = WIDE // HD
F32 = jnp.float32
BF16 = jnp.bfloat16


def dot(a, b, contract=((1,), (0,))):
    return lax.dot_general(a, b, (contract, ((), ())), preferred_element_type=F32)


def iota(shape, dim):
    return lax.broadcasted_iota(jnp.int32, shape, dim)


def positions(block, offset, rows, total):
    half = rows // 2
    return jnp.where(
        offset < half, block * half + offset, (2 * total - 1 - block) * half + offset - half
    )


def spread(columns, rows):
    lane_head = iota((rows, WIDE), 1) // HD
    out = jnp.broadcast_to(columns[QUAD - 1], (rows, WIDE))
    for i in range(QUAD - 2, -1, -1):
        out = jnp.where(lane_head == i, columns[i], out)
    return out


def kernel(
    ctx_total, exp_total, cap,
    query, key_value, prior_out, prior_lse, gain, w_gate, w_up, ids, weights,
    attended_out, hidden_out,
    q, prior, wg, wu, window, keys, values, attended, pick, send, recv,
    meta_send, meta_recv, normed, hidden,
    local_sem, kv_send, kv_recv, row_send, row_recv, meta_send_sem, meta_recv_sem,
):
    rows = q.shape[0]
    width = q.shape[1]
    chunks = width // WIDE
    span = STEPS * rows
    me = lax.axis_index("exp")
    ctx = lax.axis_index("ctx")

    loads = [
        pltpu.make_async_copy(a, b, local_sem.at[i])
        for i, (a, b) in enumerate(((query, q), (prior_out, prior), (w_gate, wg), (w_up, wu)))
    ]
    for load in loads:
        load.start()

    steps = sorted({d % ctx_total for j in range(1, STEPS) for d in (j, -j)})
    barrier = pltpu.get_barrier_semaphore()
    for d in steps:
        pl.semaphore_signal(
            barrier, inc=1, device_id={"ctx": lax.rem(ctx + d, ctx_total)}, device_id_type=MESH
        )

    def greet(d, _):
        pl.semaphore_signal(
            barrier, inc=1, device_id={"exp": lax.rem(me + d, exp_total)}, device_id_type=MESH
        )
        return 0

    lax.fori_loop(1, exp_total, greet, 0)
    pl.semaphore_wait(barrier, exp_total - 1 + len(steps))

    passes = [
        pltpu.make_async_remote_copy(
            src_ref=key_value, dst_ref=window.at[j - 1],
            send_sem=kv_send.at[j - 1], recv_sem=kv_recv.at[j - 1],
            device_id={"ctx": lax.rem(ctx + j, ctx_total)}, device_id_type=MESH,
        )
        for j in range(1, STEPS)
    ]
    for one in passes:
        one.start()

    eye = (iota((rows, rows), 0) == iota((rows, rows), 1)).astype(BF16)
    id_rows = dot(ids[...].astype(F32).astype(BF16), eye, ((0,), (0,))).astype(jnp.int32)
    weight_rows = dot(weights[...], eye, ((0,), (0,)))
    experts = iota((exp_total, rows), 0)
    named = jnp.zeros((exp_total, rows), F32)
    named_weight = jnp.zeros((exp_total, rows), F32)
    for j in range(IN_FLIGHT):
        hit = (experts == id_rows[j : j + 1, :]).astype(F32)
        named = named + hit
        named_weight = named_weight + hit * weight_rows[j : j + 1, :]
    earlier = (iota((rows, rows), 0) < iota((rows, rows), 1)).astype(BF16)
    rank = dot(named.astype(BF16), earlier).astype(jnp.int32)
    rank = jnp.where(named > 0.5, rank, -1)
    slot = iota((cap, rows), 0)
    for e in range(exp_total):
        chosen = (slot == rank[e : e + 1, :]).astype(BF16)
        pick[e * cap : (e + 1) * cap, :] = chosen
        column = jnp.sum(
            chosen.astype(F32) * named_weight[e : e + 1, :], axis=1, keepdims=True
        )
        diagonal = (iota((cap, rows), 0) == iota((cap, rows), 1)).astype(F32)
        line = jnp.sum(diagonal * column, axis=0, keepdims=True)
        meta_send[e] = jnp.broadcast_to(line, (8, rows))

    def meta_copy(to, at):
        return pltpu.make_async_remote_copy(
            src_ref=meta_send.at[to], dst_ref=meta_recv.at[at],
            send_sem=meta_send_sem.at[to], recv_sem=meta_recv_sem.at[at],
            device_id={"exp": to}, device_id_type=MESH,
        )

    def start_meta(d, _):
        meta_copy(lax.rem(me + d, exp_total), me).start()
        return 0

    lax.fori_loop(1, exp_total, start_meta, 0)
    meta_recv[me] = meta_send[me]

    own = iota((rows, 1), 0)
    query_pos = positions(ctx, own, rows, ctx_total)
    bias = []
    for j in range(STEPS):
        source = lax.rem(ctx - j + ctx_total, ctx_total)
        key_pos = positions(source, iota((1, rows), 1), rows, ctx_total)
        bias.append(jnp.where(key_pos <= query_pos, 0.0, -1e30))
    bias = jnp.concatenate(bias, axis=1)

    for one in passes:
        one.wait_recv()
    for j in range(STEPS):
        block = key_value[...] if j == 0 else window[j - 1]
        block_keys = block[:, : KVH * HD] * jnp.asarray(HD ** (-0.5), BF16)
        block_values = block[:, KVH * HD :]
        for g in range(KVH):
            for i in range(QUAD):
                row = iota((KVH * HD, WIDE), 0)
                lane = iota((KVH * HD, WIDE), 1)
                place = (
                    (row - g * HD == lane - i * HD) & (lane // HD == i)
                ).astype(BF16)
                at = i * span + j * rows
                keys[g, at : at + rows, :] = dot(block_keys, place).astype(BF16)
                values[g, at : at + rows, :] = dot(block_values, place).astype(BF16)

    loads[0].wait()
    loads[1].wait()

    def row_copy(c, to, at):
        return pltpu.make_async_remote_copy(
            src_ref=send.at[c, pl.ds(pl.multiple_of(to * cap, cap), cap)],
            dst_ref=recv.at[c, pl.ds(pl.multiple_of(at * cap, cap), cap)],
            send_sem=row_send.at[c, to], recv_sem=row_recv.at[c, at],
            device_id={"exp": to}, device_id_type=MESH,
        )

    mine = pl.ds(pl.multiple_of(me * cap, cap), cap)
    for c in range(chunks):
        lanes = slice(c * WIDE, (c + 1) * WIDE)
        g = c * QUAD // (HQ // KVH)
        scores = dot(q[:, lanes], keys[g], ((1,), (1,)))
        powers, carried, total = [], [], []
        for i in range(QUAD):
            part = scores[:, i * span : (i + 1) * span] + bias
            head = c * QUAD + i
            logs = prior_lse[:, head : head + 1]
            row_max = jnp.maximum(jnp.max(part, axis=1, keepdims=True), logs)
            power = jnp.exp(part - row_max)
            share = jnp.exp(logs - row_max)
            carried.append(share)
            total.append(share + jnp.sum(power, axis=1, keepdims=True))
            powers.append(power.astype(BF16))
        mixed = dot(jnp.concatenate(powers, axis=1), values[g])
        result = (
            spread(carried, rows) * prior[:, lanes].astype(F32) + mixed
        ) / spread(total, rows)
        result = result.astype(BF16)
        attended[:, lanes] = result
        send[c] = dot(pick[...], result).astype(BF16)

        def start_rows(d, _, c=c):
            row_copy(c, lax.rem(me + d, exp_total), me).start()
            return 0

        lax.fori_loop(1, exp_total, start_rows, 0)
        recv[c, mine, :] = send[c, mine, :]

    store = pltpu.make_async_copy(attended, attended_out, local_sem.at[0])
    store.start()

    squares = jnp.zeros((exp_total * cap, 1), F32)
    for c in range(chunks):

        def land(d, _, c=c):
            row_copy(c, me, lax.rem(me + d, exp_total)).wait_recv()
            return 0

        lax.fori_loop(1, exp_total, land, 0)
        block = recv[c].astype(F32)
        squares = squares + jnp.sum(block * block, axis=1, keepdims=True)
    inverse = lax.rsqrt(squares / width + 1e-6)
    for c in range(chunks):
        lanes = slice(c * WIDE, (c + 1) * WIDE)
        normed[:, lanes] = (recv[c].astype(F32) * inverse * gain[:, lanes]).astype(BF16)

    def land_meta(d, _):
        meta_copy(me, lax.rem(me + d, exp_total)).wait_recv()
        return 0

    lax.fori_loop(1, exp_total, land_meta, 0)
    diagonal = (iota((cap, rows), 0) == iota((cap, rows), 1)).astype(F32)
    slot_weight = jnp.concatenate(
        [
            jnp.sum(diagonal * meta_recv[s][:1, :], axis=1, keepdims=True)
            for s in range(exp_total)
        ],
        axis=0,
    )
    loads[2].wait()
    loads[3].wait()
    stores = []
    for n in range(wg.shape[1] // WIDE):
        lanes = slice(n * WIDE, (n + 1) * WIDE)
        gate = dot(normed[...], wg[:, lanes])
        up = dot(normed[...], wu[:, lanes])
        hidden[:, lanes] = (gate / (1.0 + jnp.exp(-gate)) * up * slot_weight).astype(BF16)
        out = pltpu.make_async_copy(
            hidden.at[:, lanes], hidden_out.at[:, lanes], local_sem.at[1 + n]
        )
        out.start()
        stores.append(out)

    for one in passes:
        one.wait_send()

    def sent(d, _):
        to = lax.rem(me + d, exp_total)
        meta_copy(to, me).wait_send()
        for c in range(chunks):
            row_copy(c, to, me).wait_send()
        return 0

    lax.fori_loop(1, exp_total, sent, 0)
    store.wait()
    for out in stores:
        out.wait()


def per_device(
    query, key_value, prior_out, prior_lse, norm_gain, w_gate, w_up, expert_ids, route_weight
):
    ctx_total = lax.axis_size("ctx")
    exp_total = lax.axis_size("exp")
    rows, width = query.shape[1:]
    hidden_width = w_gate.shape[2]
    capacity = max(2, IN_FLIGHT * rows * 3 // (2 * exp_total))
    cap = -(-capacity // 16) * 16
    chunks = width // WIDE
    pair_width = key_value.shape[2]
    any_space = pl.BlockSpec(memory_space=pl.ANY)
    vmem = pl.BlockSpec(memory_space=pltpu.VMEM)
    dma = pltpu.SemaphoreType.DMA
    slots = exp_total * cap
    attended, hidden = pl.pallas_call(
        functools.partial(kernel, ctx_total, exp_total, cap),
        out_shape=(
            jax.ShapeDtypeStruct((rows, width), BF16),
            jax.ShapeDtypeStruct((slots, hidden_width), BF16),
        ),
        in_specs=[any_space, vmem, any_space, vmem, vmem, any_space, any_space, vmem, vmem],
        out_specs=(any_space, any_space),
        scratch_shapes=[
            pltpu.VMEM((rows, width), BF16),
            pltpu.VMEM((rows, width), BF16),
            pltpu.VMEM(w_gate.shape[1:], BF16),
            pltpu.VMEM(w_up.shape[1:], BF16),
            pltpu.VMEM((STEPS - 1, rows, pair_width), BF16),
            pltpu.VMEM((KVH, QUAD * STEPS * rows, WIDE), BF16),
            pltpu.VMEM((KVH, QUAD * STEPS * rows, WIDE), BF16),
            pltpu.VMEM((rows, width), BF16),
            pltpu.VMEM((slots, rows), BF16),
            pltpu.VMEM((chunks, slots, WIDE), BF16),
            pltpu.VMEM((chunks, slots, WIDE), BF16),
            pltpu.VMEM((exp_total, 8, rows), F32),
            pltpu.VMEM((exp_total, 8, rows), F32),
            pltpu.VMEM((slots, width), BF16),
            pltpu.VMEM((slots, hidden_width), BF16),
            dma((8,)),
            dma((STEPS - 1,)),
            dma((STEPS - 1,)),
            dma((chunks, exp_total)),
            dma((chunks, exp_total)),
            dma((exp_total,)),
            dma((exp_total,)),
        ],
        compiler_params=pltpu.CompilerParams(
            collective_id=0, has_side_effects=True, vmem_limit_bytes=48 * 1024 * 1024
        ),
    )(
        query[0], key_value[0], prior_out[0], prior_lse[0], norm_gain[None], w_gate[0], w_up[0],
        expert_ids[0], route_weight[0],
    )
    hidden = hidden.reshape(exp_total, cap, hidden_width)[:, :capacity]
    return (attended[None], hidden.reshape(1, 1, exp_total * capacity, hidden_width))


def solution(mesh):
    placed = (
        P("exp", "ctx", None),
        P("exp", "ctx", None),
        P("exp", "ctx", None),
        P("exp", "ctx", None),
        P(),
        P("exp", None, None),
        P("exp", None, None),
        P("exp", "ctx", None),
        P("exp", "ctx", None),
    )
    return jax.shard_map(
        per_device,
        mesh=mesh,
        in_specs=placed,
        out_specs=(P("exp", "ctx", None), P("ctx", "exp", None, None)),
        check_vma=False,
    )
```

time: 117 us -> 62.5 us (0.53)
  Pallas kernels: 0 us -> 51.9 us
  waiting for transfers between devices: 39.7 us -> 0 us
  local copies, waits for them, and re-layouts: 31.3 us -> 9.5 us
  matrix products: 15.7 us -> 0 us
  starting transfers between devices: 14.6 us -> 0 us
  other arithmetic: 14.4 us -> 0 us
    pallas_call x0 -> x1, Pallas kernels: none -> 51.9 us  [per_device(): pl.pallas_call(functools.partial(kernel, ctx_total, exp_total, cap), out_...]
    all_to_all x2 -> x0, waiting for transfers between devices: 35.8 us -> none  [the longest x1 35.8 us: per_device(): lax.all_to_all(payload, 'exp', split_axis=0, concat_axis=0, tiled=True)]
    dot_general x4 -> x0, matrix products: 15.7 us -> none  [the longest x1 6.44 us: attend_local(): jnp.einsum('gqs,gsd->gqd', powers_low, value_rows, preferred_element_type...]
    all_to_all x2 -> x0, starting transfers between devices: 9.87 us -> none  [the longest x1 4.99 us: per_device(): lax.all_to_all(payload, 'exp', split_axis=0, concat_axis=0, tiled=True)]
    gather x2 -> x0, local copies, waits for them, and re-layouts: 8.88 us -> none  [the longest x1 6.18 us: per_device(): attended[clamped // IN_FLIGHT]]
    reduce_sum x4 -> x0, other arithmetic: 6.44 us -> none  [the longest x1 4.41 us: attend_local(): denominator = carried + jnp.sum(powers, axis=-1)]
    ppermute x2 -> x0, starting transfers between devices: 4.71 us -> none  [passed_along(): return lax.ppermute(block, axis, route)]
    convert_element_type x4 -> x0, other arithmetic: 4.26 us -> none  [the longest x1 2.4 us: attend_local(): return result.reshape(row_count, HQ * HD).astype(jnp.bfloat16)]
  transfers between devices with their start and end apart: 4 -> 0, of which waited for: 2 -> 0; matrix products, arithmetic and copies ran while one was open for 46% -> 0% of each run, Pallas kernels for 0% -> 0%
where the time goes in v1:
time: 62.5 us; the launch traced here: 62.1 us
  Pallas kernels  51.9 us (83%)
  local copies, waits for them, and re-layouts  9.5 us (15%)
  between operations  0.65 us (1%)
    pallas_call x1, Pallas kernels, per_device(): pl.pallas_call(functools.partial(kernel, ctx_total, exp_total, cap), out_...  51.9 us
    unnamed x15, local copies, waits for them, and re-layouts  9.5 us

profile of v1, /device:TPU:0, one launch (start us, length us, event | category | flops | bytes accessed | tf_op | source)
XLA Modules:
  0.0 62.1 jit_solution(15154491156784460248)
XLA Ops:
  0.6 0.8 %copy.13 = bf16[1,128,2]{2,1,0:T(8,128)(2,1)S(1)} copy(bf16[1,128,2]{1,2,0:T(2,128)(2,1)} %param.17) | data formatting | bytes 1024 | tf_op args[8]
  1.4 0.8 %copy.11 = f32[1,128,32]{2,1,0:T(8,128)S(1)} copy(f32[1,128,32]{1,2,0:T(8,128)} %param.12) | data formatting | bytes 32768 | tf_op args[3]
  2.2 0.8 %copy.12 = s32[1,128,2]{2,1,0:T(8,128)S(1)} copy(s32[1,128,2]{1,2,0:T(2,128)} %param.16) | data formatting | bytes 2048 | tf_op args[7]
  3.0 0.0 copy-start
  3.0 1.9 %copy-done = bf16[1,2048,768]{2,1,0:T(8,128)(2,1)S(1)} copy-done((bf16[1,2048,768]{2,1,0:T(8,128)(2,1)S(1)}, bf16[1,2048,768]{2,1,0:T(8,128)(2,1)}, u32[]{:S(2)}) %copy-start) | copy-done | bytes 3145752
  4.9 0.0 copy-start.1
  4.9 1.0 %copy-done.1 = bf16[1,128,2048]{2,1,0:T(8,128)(2,1)S(1)} copy-done((bf16[1,128,2048]{2,1,0:T(8,128)(2,1)S(1)}, bf16[1,128,2048]{2,1,0:T(8,128)(2,1)}, u32[]{:S(2)}) %copy-start.1) | copy-done | bytes 524312
  6.0 0.0 copy-start.2
  6.0 1.0 %copy-done.2 = bf16[1,128,2048]{2,1,0:T(8,128)(2,1)S(1)} copy-done((bf16[1,128,2048]{2,1,0:T(8,128)(2,1)S(1)}, bf16[1,128,2048]{2,1,0:T(8,128)(2,1)}, u32[]{:S(2)}) %copy-start.2) | copy-done | bytes 524312
  7.0 0.0 copy-start.3
  7.0 0.8 %copy-done.3 = bf16[1,128,256]{2,1,0:T(8,128)(2,1)S(1)} copy-done((bf16[1,128,256]{2,1,0:T(8,128)(2,1)S(1)}, bf16[1,128,256]{2,1,0:T(8,128)(2,1)}, u32[]{:S(2)}) %copy-start.3) | copy-done | bytes 65560
  7.8 0.0 copy-start.4
  7.8 0.7 %copy-done.4 = f32[2048]{0:T(1024)S(1)} copy-done((f32[2048]{0:T(1024)S(1)}, f32[2048]{0:T(1024)}, u32[]{:S(2)}) %copy-start.4) | copy-done | bytes 8216
  8.5 51.9 %shard_map.104 = (bf16[128,2048]{1,0:T(8,128)(2,1)S(1)}, bf16[384,768]{1,0:T(8,128)(2,1)S(1)}) custom-call(bf16[128,2048]{1,0:T(8,128)(2,1)S(1)} %bitcast.13, bf16[128,256]{1,0:T(8,128)(2,1)S(1)} %bitcast.19, bf16[128,2048]{1,0:T(8,128)(2,1)S(1)} %bitcast.14, f32[128,32]{1,0:T(8,128)S(1)} %bitcast.16, f32[1,2048]{1,0:T(1,128)S(1)} %bitcast.20, ...), custom_call_target="tpu_custom_call" | custom-call | tf_op jit(solution)/shard_map/pallas_call | solution.py:278
  60.5 0.8 %copy.16 = bf16[1,128,2048]{2,1,0:T(8,128)(2,1)} copy(bf16[1,128,2048]{2,1,0:T(8,128)(2,1)S(1)} %bitcast.15) | data formatting | bytes 1048576
  61.3 0.8 %copy.17 = bf16[1,1,384,768]{3,2,1,0:T(8,128)(2,1)} copy(bf16[1,1,384,768]{3,2,1,0:T(8,128)(2,1)S(1)} %bitcast.12) | data formatting | bytes 1179648
Async XLA Ops:
  3.0 1.9 %copy-start = (bf16[1,2048,768]{2,1,0:T(8,128)(2,1)S(1)}, bf16[1,2048,768]{2,1,0:T(8,128)(2,1)}, u32[]{:S(2)}) copy-start(bf16[1,2048,768]{2,1,0:T(8,128)(2,1)} %param.14) | copy-start | bytes 9437188
  4.9 1.0 %copy-start.1 = (bf16[1,128,2048]{2,1,0:T(8,128)(2,1)S(1)}, bf16[1,128,2048]{2,1,0:T(8,128)(2,1)}, u32[]{:S(2)}) copy-start(bf16[1,128,2048]{2,1,0:T(8,128)(2,1)} %param.9) | copy-start | bytes 1572868
  6.0 1.0 %copy-start.2 = (bf16[1,128,2048]{2,1,0:T(8,128)(2,1)S(1)}, bf16[1,128,2048]{2,1,0:T(8,128)(2,1)}, u32[]{:S(2)}) copy-start(bf16[1,128,2048]{2,1,0:T(8,128)(2,1)} %param.11) | copy-start | bytes 1572868
  7.0 0.8 %copy-start.3 = (bf16[1,128,256]{2,1,0:T(8,128)(2,1)S(1)}, bf16[1,128,256]{2,1,0:T(8,128)(2,1)}, u32[]{:S(2)}) copy-start(bf16[1,128,256]{2,1,0:T(8,128)(2,1)} %param.10) | copy-start | bytes 196612
  7.8 0.7 %copy-start.4 = (f32[2048]{0:T(1024)S(1)}, f32[2048]{0:T(1024)}, u32[]{:S(2)}) copy-start(f32[2048]{0:T(1024)} %param.13) | copy-start | bytes 24580

commit v2 on v1

v2 whole, which is shorter than its diff:
```python
import functools

import jax
import jax.numpy as jnp
from jax import lax
from jax.experimental import pallas as pl
from jax.experimental.pallas import tpu as pltpu
from jax.sharding import PartitionSpec as P

HQ = 32
KVH = 2
HD = 64
FF = 768
STEPS = 3
IN_FLIGHT = 2

MESH = pl.DeviceIdType.MESH
WIDE = 256
QUAD = WIDE // HD
F32 = jnp.float32
BF16 = jnp.bfloat16


def dot(a, b, contract=((1,), (0,))):
    return lax.dot_general(a, b, (contract, ((), ())), preferred_element_type=F32)


def iota(shape, dim):
    return lax.broadcasted_iota(jnp.int32, shape, dim)


def positions(block, offset, rows, total):
    half = rows // 2
    return jnp.where(
        offset < half, block * half + offset, (2 * total - 1 - block) * half + offset - half
    )


def spread(columns, rows):
    lane_head = iota((rows, WIDE), 1) // HD
    out = jnp.broadcast_to(columns[QUAD - 1], (rows, WIDE))
    for i in range(QUAD - 2, -1, -1):
        out = jnp.where(lane_head == i, columns[i], out)
    return out


def each(first, last, body):
    if last - first <= 8:
        for d in range(first, last):
            body(d)
    else:
        lax.fori_loop(first, last, lambda d, _: (body(d), 0)[1], 0)


def slot_rows(rank_ref, base, count, cap, rows):
    slot = iota((cap, rows), 0).astype(F32)
    return jnp.concatenate(
        [(slot == rank_ref[pl.ds(base + e, 1), :]).astype(BF16) for e in range(count)], axis=0
    )


def kernel(
    ctx_total, exp_total, cap,
    query, key_value, prior_out, prior_lse, gain, w_gate, w_up, ids, weights,
    attended_out, hidden_out,
    q, kv, prior, lse, scale, wg, wu, id_rows, weight_rows,
    window, keys, values, raw, pick, relay_pick, send, relay_in, relay_out, recv,
    rank_send, rank_recv, meta_send, meta_recv, normed, hidden,
    local_sem, out_sem, kv_send, kv_recv, row_send, row_recv, relay_send,
    raw_send, raw_recv, rank_sems, meta_send_sem, meta_recv_sem,
):
    rows = q.shape[0]
    width = q.shape[1]
    chunks = width // WIDE
    span = STEPS * rows
    half = exp_total // 2
    me = lax.axis_index("exp")
    ctx = lax.axis_index("ctx")
    side = me // half
    base = side * half
    local = me - base
    far = half - base
    across = lax.rem(me + half, exp_total)

    loads = [
        pltpu.make_async_copy(a, b, local_sem.at[i])
        for i, (a, b) in enumerate(
            (
                (key_value, kv), (ids, id_rows), (weights, weight_rows), (prior_lse, lse),
                (query, q), (prior_out, prior), (gain, scale), (w_gate, wg), (w_up, wu),
            )
        )
    ]
    for load in loads:
        load.start()

    steps = sorted({d % ctx_total for j in range(1, STEPS) for d in (j, -j)})
    barrier = pltpu.get_barrier_semaphore()
    for d in steps:
        pl.semaphore_signal(
            barrier, inc=1, device_id={"ctx": lax.rem(ctx + d, ctx_total)}, device_id_type=MESH
        )

    def greet(d):
        pl.semaphore_signal(
            barrier, inc=1, device_id={"exp": lax.rem(me + d, exp_total)}, device_id_type=MESH
        )

    each(1, exp_total, greet)

    loads[1].wait()
    loads[2].wait()
    experts = iota((exp_total, rows), 0)
    named = jnp.zeros((exp_total, rows), F32)
    named_weight = jnp.zeros((exp_total, rows), F32)
    for j in range(IN_FLIGHT):
        hit = (experts == id_rows[j : j + 1, :]).astype(F32)
        named = named + hit
        named_weight = named_weight + hit * weight_rows[j : j + 1, :].astype(F32)
    earlier = (iota((rows, rows), 0) < iota((rows, rows), 1)).astype(BF16)
    rank_send[...] = jnp.where(named > 0.5, dot(named.astype(BF16), earlier), -1.0)
    loads[0].wait()
    pl.semaphore_wait(barrier, exp_total - 1 + len(steps))

    passes = [
        pltpu.make_async_remote_copy(
            src_ref=kv, dst_ref=window.at[j - 1],
            send_sem=kv_send.at[j - 1], recv_sem=kv_recv.at[j - 1],
            device_id={"ctx": lax.rem(ctx + j, ctx_total)}, device_id_type=MESH,
        )
        for j in range(1, STEPS)
    ]
    for one in passes:
        one.start()
    rank_copy = pltpu.make_async_remote_copy(
        src_ref=rank_send, dst_ref=rank_recv, send_sem=rank_sems.at[0],
        recv_sem=rank_sems.at[1], device_id={"exp": across}, device_id_type=MESH,
    )
    rank_copy.start()
    pick[...] = slot_rows(rank_send, base, half, cap, rows)

    own = iota((rows, 1), 0)
    query_pos = positions(ctx, own, rows, ctx_total)
    bias = []
    for j in range(STEPS):
        source = lax.rem(ctx - j + ctx_total, ctx_total)
        key_pos = positions(source, iota((1, rows), 1), rows, ctx_total)
        bias.append(jnp.where(key_pos <= query_pos, 0.0, -1e30))
    bias = jnp.concatenate(bias, axis=1)

    place_row = iota((KVH * HD, WIDE), 0)
    place_lane = lax.rem(iota((KVH * HD, WIDE), 1), HD)
    places = [(place_row == place_lane + g * HD).astype(BF16) for g in range(KVH)]
    lane_head = iota((rows, WIDE), 1) // HD

    def lay_out(j, block):
        block_keys = block[:, : KVH * HD] * jnp.asarray(HD ** (-0.5), BF16)
        block_values = block[:, KVH * HD :]
        for g in range(KVH):
            for part, target in ((block_keys, keys), (block_values, values)):
                tiled = dot(part, places[g])
                for i in range(QUAD):
                    at = i * span + j * rows
                    target[g, at : at + rows, :] = jnp.where(lane_head == i, tiled, 0.0).astype(BF16)

    lay_out(0, kv[...])
    loads[3].wait()
    logs_all = jnp.transpose(lse[...])
    loads[4].wait()
    loads[5].wait()
    for j in range(1, STEPS):
        passes[j - 1].wait_recv()
        lay_out(j, window[j - 1])

    def slots_of(index):
        return pl.ds(pl.multiple_of(index * cap, cap), cap)

    def row_copy(c, to_local, source_ref, sems, source):
        return pltpu.make_async_remote_copy(
            src_ref=source_ref.at[c, slots_of(to_local)],
            dst_ref=recv.at[c, slots_of(source)],
            send_sem=sems.at[c, to_local], recv_sem=row_recv.at[c, source],
            device_id={"exp": base + to_local}, device_id_type=MESH,
        )

    def peer(d):
        return lax.rem(local + d, half)

    def raw_copy(c):
        return pltpu.make_async_remote_copy(
            src_ref=raw.at[c], dst_ref=relay_in.at[c], send_sem=raw_send.at[c],
            recv_sem=raw_recv.at[c], device_id={"exp": across}, device_id_type=MESH,
        )

    def out_copy(c):
        return pltpu.make_async_copy(
            raw.at[c], attended_out.at[:, c * WIDE : (c + 1) * WIDE], out_sem.at[c]
        )

    def meta_copy(to, at):
        return pltpu.make_async_remote_copy(
            src_ref=meta_send.at[to], dst_ref=meta_recv.at[at],
            send_sem=meta_send_sem.at[to], recv_sem=meta_recv_sem.at[at],
            device_id={"exp": to}, device_id_type=MESH,
        )

    def pass_on(c):
        raw_copy(c).wait_recv()
        relay_out[c] = dot(relay_pick[...], relay_in[c]).astype(BF16)
        each(1, half, lambda d: row_copy(c, peer(d), relay_out, relay_send, across).start())
        recv[c, slots_of(across), :] = relay_out[c, slots_of(local), :]

    diagonal = (iota((cap, rows), 0) == iota((cap, rows), 1)).astype(F32)

    def send_weights():
        slot = iota((cap, rows), 0).astype(F32)
        for e in range(exp_total):
            chosen = slot == rank_send[e : e + 1, :]
            column = jnp.sum(
                jnp.where(chosen, named_weight[e : e + 1, :], 0.0), axis=1, keepdims=True
            )
            line = jnp.sum(diagonal * column, axis=0, keepdims=True)
            meta_send[e] = jnp.broadcast_to(line, (8, rows))
        each(1, exp_total, lambda d: meta_copy(lax.rem(me + d, exp_total), me).start())
        meta_recv[me] = meta_send[me]

    def scores_of(c):
        g = c * QUAD // (HQ // KVH)
        return dot(q[:, c * WIDE : (c + 1) * WIDE], keys[g], ((1,), (1,)))

    lag = 2
    ahead = scores_of(0)
    for c in range(chunks):
        lanes = slice(c * WIDE, (c + 1) * WIDE)
        g = c * QUAD // (HQ // KVH)
        scores = ahead
        if c + 1 < chunks:
            ahead = scores_of(c + 1)
        powers, carried, total = [], [], []
        for i in range(QUAD):
            part = scores[:, i * span : (i + 1) * span] + bias
            head = c * QUAD + i
            logs = logs_all[:, head : head + 1]
            row_max = jnp.maximum(jnp.max(part, axis=1, keepdims=True), logs)
            power = jnp.exp(part - row_max)
            share = jnp.exp(logs - row_max)
            carried.append(share)
            total.append(share + jnp.sum(power, axis=1, keepdims=True))
            powers.append(power.astype(BF16))
        mixed = dot(jnp.concatenate(powers, axis=1), values[g])
        result = (
            spread(carried, rows) * prior[:, lanes].astype(F32) + mixed
        ) / spread(total, rows)
        result = result.astype(BF16)
        raw[c] = result
        raw_copy(c).start()
        send[c] = dot(pick[...], result).astype(BF16)
        each(1, half, lambda d: row_copy(c, peer(d), send, row_send, me).start())
        out_copy(c).start()
        recv[c, slots_of(me), :] = send[c, slots_of(local), :]
        if c == 0:
            rank_copy.wait_recv()
            relay_pick[...] = slot_rows(rank_recv, base, half, cap, rows)
        if c == 1:
            send_weights()
        if c >= lag:
            pass_on(c - lag)
    for c in range(max(0, chunks - lag), chunks):
        pass_on(c)

    loads[6].wait()
    loads[7].wait()
    loads[8].wait()
    stores = []
    for order, start in enumerate((base, far)):
        block_rows = pl.ds(pl.multiple_of(start * cap, cap), half * cap)

        def land(d, start=start, order=order):
            if order == 0:
                source = base + peer(d)
            else:
                source = far + lax.rem(local + d, half)
            meta_copy(me, source).wait_recv()
            for c in range(chunks):
                row_copy(c, local, send, row_send, source).wait_recv()

        each(1, half, land)
        if order == 1:
            meta_copy(me, across).wait_recv()
        squares = jnp.zeros((half * cap, 1), F32)
        for c in range(chunks):
            block = recv[c, block_rows, :].astype(F32)
            squares = squares + jnp.sum(block * block, axis=1, keepdims=True)
        inverse = lax.rsqrt(squares / width + 1e-6)
        for c in range(chunks):
            lanes = slice(c * WIDE, (c + 1) * WIDE)
            block = recv[c, block_rows, :].astype(F32)
            normed[:, lanes] = (block * inverse * scale[:, lanes]).astype(BF16)
        slot_weight = jnp.concatenate(
            [
                jnp.sum(diagonal * meta_recv[start + s][:1, :], axis=1, keepdims=True)
                for s in range(half)
            ],
            axis=0,
        )
        for n in range(wg.shape[1] // WIDE):
            lanes = slice(n * WIDE, (n + 1) * WIDE)
            gate = dot(normed[...], wg[:, lanes])
            up = dot(normed[...], wu[:, lanes])
            hidden[order, :, lanes] = (
                gate / (1.0 + jnp.exp(-gate)) * up * slot_weight
            ).astype(BF16)
        out = pltpu.make_async_copy(
            hidden.at[order], hidden_out.at[block_rows], local_sem.at[order]
        )
        out.start()
        stores.append(out)

    for one in passes:
        one.wait_send()
    rank_copy.wait_send()
    each(1, exp_total, lambda d: meta_copy(lax.rem(me + d, exp_total), me).wait_send())
    for c in range(chunks):
        raw_copy(c).wait_send()
        out_copy(c).wait()

    def sent(d):
        for c in range(chunks):
            row_copy(c, peer(d), send, row_send, me).wait_send()
            row_copy(c, peer(d), relay_out, relay_send, across).wait_send()

    each(1, half, sent)
    for out in stores:
        out.wait()


def per_device(
    query, key_value, prior_out, prior_lse, norm_gain, w_gate, w_up, expert_ids, route_weight
):
    ctx_total = lax.axis_size("ctx")
    exp_total = lax.axis_size("exp")
    rows, width = query.shape[1:]
    hidden_width = w_gate.shape[2]
    capacity = max(2, IN_FLIGHT * rows * 3 // (2 * exp_total))
    cap = -(-capacity // 16) * 16
    chunks = width // WIDE
    pair_width = key_value.shape[2]
    any_space = pl.BlockSpec(memory_space=pl.ANY)
    dma = pltpu.SemaphoreType.DMA
    slots = exp_total * cap
    half_slots = exp_total // 2 * cap
    attended, hidden = pl.pallas_call(
        functools.partial(kernel, ctx_total, exp_total, cap),
        out_shape=(
            jax.ShapeDtypeStruct((rows, width), BF16),
            jax.ShapeDtypeStruct((slots, hidden_width), BF16),
        ),
        in_specs=[any_space] * 9,
        out_specs=(any_space, any_space),
        scratch_shapes=[
            pltpu.VMEM((rows, width), BF16),
            pltpu.VMEM((rows, pair_width), BF16),
            pltpu.VMEM((rows, width), BF16),
            pltpu.VMEM((HQ, rows), F32),
            pltpu.VMEM((1, width), F32),
            pltpu.VMEM(w_gate.shape[1:], BF16),
            pltpu.VMEM(w_up.shape[1:], BF16),
            pltpu.VMEM((IN_FLIGHT, rows), jnp.int32),
            pltpu.VMEM((IN_FLIGHT, rows), BF16),
            pltpu.VMEM((STEPS - 1, rows, pair_width), BF16),
            pltpu.VMEM((KVH, QUAD * STEPS * rows, WIDE), BF16),
            pltpu.VMEM((KVH, QUAD * STEPS * rows, WIDE), BF16),
            pltpu.VMEM((chunks, rows, WIDE), BF16),
            pltpu.VMEM((half_slots, rows), BF16),
            pltpu.VMEM((half_slots, rows), BF16),
            pltpu.VMEM((chunks, half_slots, WIDE), BF16),
            pltpu.VMEM((chunks, rows, WIDE), BF16),
            pltpu.VMEM((chunks, half_slots, WIDE), BF16),
            pltpu.VMEM((chunks, slots, WIDE), BF16),
            pltpu.VMEM((exp_total, rows), F32),
            pltpu.VMEM((exp_total, rows), F32),
            pltpu.VMEM((exp_total, 8, rows), F32),
            pltpu.VMEM((exp_total, 8, rows), F32),
            pltpu.VMEM((half_slots, width), BF16),
            pltpu.VMEM((2, half_slots, hidden_width), BF16),
            dma((9,)),
            dma((chunks,)),
            dma((STEPS - 1,)),
            dma((STEPS - 1,)),
            dma((chunks, exp_total // 2)),
            dma((chunks, exp_total)),
            dma((chunks, exp_total // 2)),
            dma((chunks,)),
            dma((chunks,)),
            dma((2,)),
            dma((exp_total,)),
            dma((exp_total,)),
        ],
        compiler_params=pltpu.CompilerParams(
            collective_id=0, has_side_effects=True, vmem_limit_bytes=60 * 1024 * 1024
        ),
    )(
        query[0], key_value[0], prior_out[0], prior_lse[0].T, norm_gain[None], w_gate[0], w_up[0],
        expert_ids[0].T, route_weight[0].T,
    )
    hidden = hidden.reshape(exp_total, cap, hidden_width)[:, :capacity]
    return (attended[None], hidden.reshape(1, 1, exp_total * capacity, hidden_width))


def solution(mesh):
    placed = (
        P("exp", "ctx", None),
        P("exp", "ctx", None),
        P("exp", "ctx", None),
        P("exp", "ctx", None),
        P(),
        P("exp", None, None),
        P("exp", None, None),
        P("exp", "ctx", None),
        P("exp", "ctx", None),
    )
    return jax.shard_map(
        per_device,
        mesh=mesh,
        in_specs=placed,
        out_specs=(P("exp", "ctx", None), P("ctx", "exp", None, None)),
        check_vma=False,
    )
```

time: 62.5 us -> 50.3 us (0.80)
  Pallas kernels: 51.9 us -> 45.6 us
  local copies, waits for them, and re-layouts: 9.5 us -> 3.8 us
    pallas_call x1, Pallas kernels: 51.9 us -> 45.6 us  [per_device(): pl.pallas_call(functools.partial(kernel, ctx_total, exp_total, cap), out_...]
    unnamed x15 -> x2, local copies, waits for them, and re-layouts: 9.5 us -> 3.8 us
where the time goes in v2:
time: 50.3 us; the launch traced here: 50.1 us
  Pallas kernels  45.6 us (91%)
  local copies, waits for them, and re-layouts  3.8 us (8%)
  between operations  0.64 us (1%)
    pallas_call x1, Pallas kernels, per_device(): pl.pallas_call(functools.partial(kernel, ctx_total, exp_total, cap), out_...  45.6 us
    unnamed x2, local copies, waits for them, and re-layouts  3.8 us

profile of v2, /device:TPU:0, one launch (start us, length us, event | category | flops | bytes accessed | tf_op | source)
XLA Modules:
  0.0 50.1 jit_solution(9987516989054346942)
XLA Ops:
  0.6 45.6 %shard_map.104 = (bf16[128,2048]{1,0:T(8,128)(2,1)}, bf16[384,768]{1,0:T(8,128)(2,1)}) custom-call(bf16[128,2048]{1,0:T(8,128)(2,1)} %bitcast.20, bf16[128,256]{1,0:T(8,128)(2,1)} %bitcast.23, bf16[128,2048]{1,0:T(8,128)(2,1)} %bitcast.21, f32[32,128]{1,0:T(8,128)} %bitcast.24, f32[1,2048]{1,0:T(1,128)} %bitcast.25, bf16[2048,768]{1,0:T(8,128)(2,1)} %bitcast.17, ...), custom_call_target="tpu_custom_call" | custom-call | tf_op jit(solution)/shard_map/pallas_call | solution.py:352
  46.3 1.9 %copy.13 = bf16[1,128,2048]{2,1,0:T(8,128)(2,1)} copy(bf16[1,128,2048]{2,1,0:T(8,128)(2,1)} %bitcast.22) | data formatting | bytes 1048576
  48.2 1.9 %copy.14 = bf16[1,1,384,768]{3,2,1,0:T(8,128)(2,1)} copy(bf16[1,1,384,768]{3,2,1,0:T(8,128)(2,1)} %bitcast.19) | data formatting | bytes 1179648

commit v3 on v2

--- a/solution.py
+++ b/solution.py
@@ -17,6 +17,7 @@
 MESH = pl.DeviceIdType.MESH
 WIDE = 256
 QUAD = WIDE // HD
+PIECES = 4
 F32 = jnp.float32
 BF16 = jnp.bfloat16
 
@@ -65,7 +66,7 @@
     attended_out, hidden_out,
     q, kv, prior, lse, scale, wg, wu, id_rows, weight_rows,
     window, keys, values, raw, pick, relay_pick, send, relay_in, relay_out, recv,
-    rank_send, rank_recv, meta_send, meta_recv, normed, hidden,
+    rank_send, rank_recv, meta_send, meta_recv, squares, gates, ups, hidden,
     local_sem, out_sem, kv_send, kv_recv, row_send, row_recv, relay_send,
     raw_send, raw_recv, rank_sems, meta_send_sem, meta_recv_sem,
 ):
@@ -153,24 +154,24 @@
     places = [(place_row == place_lane + g * HD).astype(BF16) for g in range(KVH)]
     lane_head = iota((rows, WIDE), 1) // HD
 
-    def lay_out(j, block):
+    def lay_out(g, j):
+        block = kv[...] if j == 0 else window[j - 1]
         block_keys = block[:, : KVH * HD] * jnp.asarray(HD ** (-0.5), BF16)
         block_values = block[:, KVH * HD :]
-        for g in range(KVH):
-            for part, target in ((block_keys, keys), (block_values, values)):
-                tiled = dot(part, places[g])
-                for i in range(QUAD):
-                    at = i * span + j * rows
-                    target[g, at : at + rows, :] = jnp.where(lane_head == i, tiled, 0.0).astype(BF16)
-
-    lay_out(0, kv[...])
+        for part, target in ((block_keys, keys), (block_values, values)):
+            tiled = dot(part, places[g])
+            for i in range(QUAD):
+                at = i * span + j * rows
+                target[g, at : at + rows, :] = jnp.where(lane_head == i, tiled, 0.0).astype(BF16)
+
+    lay_out(0, 0)
     loads[3].wait()
     logs_all = jnp.transpose(lse[...])
     loads[4].wait()
     loads[5].wait()
     for j in range(1, STEPS):
         passes[j - 1].wait_recv()
-        lay_out(j, window[j - 1])
+        lay_out(0, j)
 
     def slots_of(index):
         return pl.ds(pl.multiple_of(index * cap, cap), cap)
@@ -228,14 +229,55 @@
         g = c * QUAD // (HQ // KVH)
         return dot(q[:, c * WIDE : (c + 1) * WIDE], keys[g], ((1,), (1,)))
 
-    lag = 2
-    ahead = scores_of(0)
-    for c in range(chunks):
+    def absorb(order, c):
+        start = (base, far)[order]
+        block_rows = pl.ds(pl.multiple_of(start * cap, cap), half * cap)
+        each(
+            1, half,
+            lambda d: row_copy(c, local, send, row_send, start + peer(d)).wait_recv(),
+        )
+        block = recv[c, block_rows, :].astype(F32)
+        square = jnp.sum(block * block, axis=1, keepdims=True)
         lanes = slice(c * WIDE, (c + 1) * WIDE)
-        g = c * QUAD // (HQ // KVH)
-        scores = ahead
-        if c + 1 < chunks:
-            ahead = scores_of(c + 1)
+        scaled = (block * scale[:, lanes]).astype(BF16)
+        gate = dot(scaled, wg[lanes, :])
+        up = dot(scaled, wu[lanes, :])
+        if c == 0:
+            squares[order] = square
+            gates[order] = gate
+            ups[order] = up
+        else:
+            squares[order] += square
+            gates[order] += gate
+            ups[order] += up
+
+    def finish(order):
+        start = (base, far)[order]
+        each(1, half, lambda d: meta_copy(me, start + peer(d)).wait_recv())
+        if order == 1:
+            meta_copy(me, across).wait_recv()
+        slot_weight = jnp.concatenate(
+            [
+                jnp.sum(diagonal * meta_recv[start + s][:1, :], axis=1, keepdims=True)
+                for s in range(half)
+            ],
+            axis=0,
+        )
+        inverse = lax.rsqrt(squares[order] / width + 1e-6)
+        gate = gates[order] * inverse
+        weight = inverse * slot_weight
+        hidden[order] = (gate / (1.0 + jnp.exp(-gate)) * (ups[order] * weight)).astype(BF16)
+        block_rows = pl.ds(pl.multiple_of(start * cap, cap), half * cap)
+        out = pltpu.make_async_copy(
+            hidden.at[order], hidden_out.at[block_rows], local_sem.at[order]
+        )
+        out.start()
+        return out
+
+    heads_per_key = HQ // KVH
+    def attend(c, scores):
+        lanes = slice(c * WIDE, (c + 1) * WIDE)
+        g = c * QUAD // heads_per_key
         powers, carried, total = [], [], []
         for i in range(QUAD):
             part = scores[:, i * span : (i + 1) * span] + bias
@@ -258,63 +300,36 @@
         each(1, half, lambda d: row_copy(c, peer(d), send, row_send, me).start())
         out_copy(c).start()
         recv[c, slots_of(me), :] = send[c, slots_of(local), :]
+
+    lag, near_lag, far_lag = 2, 3, 5
+    ahead = scores_of(0)
+    for c in range(chunks + far_lag):
+        if c < chunks:
+            scores = ahead
+            if c + 1 < chunks:
+                if (c + 1) * QUAD % heads_per_key == 0:
+                    for j in range(STEPS):
+                        lay_out((c + 1) * QUAD // heads_per_key, j)
+                ahead = scores_of(c + 1)
+            attend(c, scores)
         if c == 0:
             rank_copy.wait_recv()
             relay_pick[...] = slot_rows(rank_recv, base, half, cap, rows)
         if c == 1:
             send_weights()
-        if c >= lag:
+        if 0 <= c - lag < chunks:
             pass_on(c - lag)
-    for c in range(max(0, chunks - lag), chunks):
-        pass_on(c)
-
-    loads[6].wait()
-    loads[7].wait()
-    loads[8].wait()
-    stores = []
-    for order, start in enumerate((base, far)):
-        block_rows = pl.ds(pl.multiple_of(start * cap, cap), half * cap)
-
-        def land(d, start=start, order=order):
-            if order == 0:
-                source = base + peer(d)
-            else:
-                source = far + lax.rem(local + d, half)
-            meta_copy(me, source).wait_recv()
-            for c in range(chunks):
-                row_copy(c, local, send, row_send, source).wait_recv()
-
-        each(1, half, land)
-        if order == 1:
-            meta_copy(me, across).wait_recv()
-        squares = jnp.zeros((half * cap, 1), F32)
-        for c in range(chunks):
-            block = recv[c, block_rows, :].astype(F32)
-            squares = squares + jnp.sum(block * block, axis=1, keepdims=True)
-        inverse = lax.rsqrt(squares / width + 1e-6)
-        for c in range(chunks):
-            lanes = slice(c * WIDE, (c + 1) * WIDE)
-            block = recv[c, block_rows, :].astype(F32)
-            normed[:, lanes] = (block * inverse * scale[:, lanes]).astype(BF16)
-        slot_weight = jnp.concatenate(
-            [
-                jnp.sum(diagonal * meta_recv[start + s][:1, :], axis=1, keepdims=True)
-                for s in range(half)
-            ],
-            axis=0,
-        )
-        for n in range(wg.shape[1] // WIDE):
-            lanes = slice(n * WIDE, (n + 1) * WIDE)
-            gate = dot(normed[...], wg[:, lanes])
-            up = dot(normed[...], wu[:, lanes])
-            hidden[order, :, lanes] = (
-                gate / (1.0 + jnp.exp(-gate)) * up * slot_weight
-            ).astype(BF16)
-        out = pltpu.make_async_copy(
-            hidden.at[order], hidden_out.at[block_rows], local_sem.at[order]
-        )
-        out.start()
-        stores.append(out)
+        if c == near_lag:
+            loads[6].wait()
+            loads[7].wait()
+            loads[8].wait()
+        if 0 <= c - near_lag < chunks:
+            absorb(0, c - near_lag)
+        if c - near_lag == chunks - 1:
+            stores = [finish(0)]
+        if 0 <= c - far_lag < chunks:
+            absorb(1, c - far_lag)
+    stores.append(finish(1))
 
     for one in passes:
         one.wait_send()
@@ -332,6 +347,21 @@
     each(1, half, sent)
     for out in stores:
         out.wait()
+
+
+def hand_over(attended, hidden, attended_out, hidden_out, sems):
+    copies = []
+    for k, (source, target) in enumerate(((attended, attended_out), (hidden, hidden_out))):
+        step = source.shape[0] // PIECES
+        for i in range(PIECES):
+            part = pl.ds(i * step, step)
+            copies.append(
+                pltpu.make_async_copy(source.at[part], target.at[part], sems.at[k, i])
+            )
+    for one in copies:
+        one.start()
+    for one in copies:
+        one.wait()
 
 
 def per_device(
@@ -381,7 +411,9 @@
             pltpu.VMEM((exp_total, rows), F32),
             pltpu.VMEM((exp_total, 8, rows), F32),
             pltpu.VMEM((exp_total, 8, rows), F32),
-            pltpu.VMEM((half_slots, width), BF16),
+            pltpu.VMEM((2, half_slots, 1), F32),
+            pltpu.VMEM((2, half_slots, hidden_width), F32),
+            pltpu.VMEM((2, half_slots, hidden_width), F32),
             pltpu.VMEM((2, half_slots, hidden_width), BF16),
             dma((9,)),
             dma((chunks,)),
@@ -403,6 +435,17 @@
         query[0], key_value[0], prior_out[0], prior_lse[0].T, norm_gain[None], w_gate[0], w_up[0],
         expert_ids[0].T, route_weight[0].T,
     )
+    attended, hidden = pl.pallas_call(
+        hand_over,
+        out_shape=(
+            jax.ShapeDtypeStruct((rows, width), BF16),
+            jax.ShapeDtypeStruct((slots, hidden_width), BF16),
+        ),
+        in_specs=[any_space] * 2,
+        out_specs=(any_space, any_space),
+        scratch_shapes=[dma((2, PIECES))],
+        compiler_params=pltpu.CompilerParams(vmem_limit_bytes=60 * 1024 * 1024),
+    )(attended, hidden)
     hidden = hidden.reshape(exp_total, cap, hidden_width)[:, :capacity]
     return (attended[None], hidden.reshape(1, 1, exp_total * capacity, hidden_width))
 

time: 50.3 us -> 80.2 us (1.59)
  Pallas kernels: 45.6 us -> 79.5 us
  local copies, waits for them, and re-layouts: 3.8 us -> 0 us
    pallas_call x0 -> x1, Pallas kernels: none -> 34.9 us  [per_device(): pl.pallas_call(hand_over, out_shape=(jax.ShapeDtypeStruct((rows, width),...]
    unnamed x2 -> x0, local copies, waits for them, and re-layouts: 3.8 us -> none
    pallas_call x1, Pallas kernels: 45.6 us -> 44.5 us  [per_device(): pl.pallas_call(functools.partial(kernel, ctx_total, exp_total, cap), out_...]
where the time goes in v3:
time: 80.2 us; the launch traced here: 80.1 us
  Pallas kernels  79.5 us (99%)
    pallas_call x1, Pallas kernels, per_device(): pl.pallas_call(functools.partial(kernel, ctx_total, exp_total, cap), out_...  44.5 us
    pallas_call x1, Pallas kernels, per_device(): pl.pallas_call(hand_over, out_shape=(jax.ShapeDtypeStruct((rows, width),...  34.9 us

profile of v3, /device:TPU:0, one launch (start us, length us, event | category | flops | bytes accessed | tf_op | source)
XLA Modules:
  0.0 80.1 jit_solution(3499196386494472022)
XLA Ops:
  0.6 44.5 %shard_map.104 = (bf16[128,2048]{1,0:T(8,128)(2,1)}, bf16[384,768]{1,0:T(8,128)(2,1)}) custom-call(bf16[128,2048]{1,0:T(8,128)(2,1)} %bitcast.19, bf16[128,256]{1,0:T(8,128)(2,1)} %bitcast.21, bf16[128,2048]{1,0:T(8,128)(2,1)} %bitcast.20, f32[32,128]{1,0:T(8,128)} %bitcast.22, f32[1,2048]{1,0:T(1,128)} %bitcast.23, bf16[2048,768]{1,0:T(8,128)(2,1)} %bitcast.17, ...), custom_call_target="tpu_custom_call" | custom-call | tf_op jit(solution)/shard_map/pallas_call | solution.py:382
  45.2 34.9 %shard_map.105 = (bf16[128,2048]{1,0:T(8,128)(2,1)}, bf16[384,768]{1,0:T(8,128)(2,1)}) custom-call(bf16[128,2048]{1,0:T(8,128)(2,1)} %get-tuple-element.6.attended, bf16[384,768]{1,0:T(8,128)(2,1)} %get-tuple-element.7.hidden), custom_call_target="tpu_custom_call" | custom-call | tf_op jit(solution)/shard_map/pallas_call | solution.py:438

commit v4 on v3

--- a/solution.py
+++ b/solution.py
@@ -35,14 +35,6 @@
     return jnp.where(
         offset < half, block * half + offset, (2 * total - 1 - block) * half + offset - half
     )
-
-
-def spread(columns, rows):
-    lane_head = iota((rows, WIDE), 1) // HD
-    out = jnp.broadcast_to(columns[QUAD - 1], (rows, WIDE))
-    for i in range(QUAD - 2, -1, -1):
-        out = jnp.where(lane_head == i, columns[i], out)
-    return out
 
 
 def each(first, last, body):
@@ -73,7 +65,6 @@
     rows = q.shape[0]
     width = q.shape[1]
     chunks = width // WIDE
-    span = STEPS * rows
     half = exp_total // 2
     me = lax.axis_index("exp")
     ctx = lax.axis_index("ctx")
@@ -148,30 +139,32 @@
         key_pos = positions(source, iota((1, rows), 1), rows, ctx_total)
         bias.append(jnp.where(key_pos <= query_pos, 0.0, -1e30))
     bias = jnp.concatenate(bias, axis=1)
+    bias = jnp.concatenate([bias] * QUAD, axis=0)
 
     place_row = iota((KVH * HD, WIDE), 0)
-    place_lane = lax.rem(iota((KVH * HD, WIDE), 1), HD)
-    places = [(place_row == place_lane + g * HD).astype(BF16) for g in range(KVH)]
+    place_lane = iota((KVH * HD, WIDE), 1)
     lane_head = iota((rows, WIDE), 1) // HD
-
-    def lay_out(g, j):
+    lane = iota((rows, WIDE // 2), 1)
+
+    def lay_out(j):
         block = kv[...] if j == 0 else window[j - 1]
         block_keys = block[:, : KVH * HD] * jnp.asarray(HD ** (-0.5), BF16)
         block_values = block[:, KVH * HD :]
-        for part, target in ((block_keys, keys), (block_values, values)):
-            tiled = dot(part, places[g])
-            for i in range(QUAD):
-                at = i * span + j * rows
-                target[g, at : at + rows, :] = jnp.where(lane_head == i, tiled, 0.0).astype(BF16)
-
-    lay_out(0, 0)
+        at = slice(j * rows, (j + 1) * rows)
+        for g in range(KVH):
+            place = (place_row == lax.rem(place_lane, HD) + g * HD).astype(BF16)
+            keys[g, at, :] = dot(block_keys, place).astype(BF16)
+            tiled = dot(block_values, place)
+            values[g, at, :] = jnp.where(lane_head < QUAD // 2, tiled, 1.0).astype(BF16)
+
+    lay_out(0)
     loads[3].wait()
     logs_all = jnp.transpose(lse[...])
     loads[4].wait()
     loads[5].wait()
     for j in range(1, STEPS):
         passes[j - 1].wait_recv()
-        lay_out(0, j)
+        lay_out(j)
 
     def slots_of(index):
         return pl.ds(pl.multiple_of(index * cap, cap), cap)
@@ -226,8 +219,26 @@
         meta_recv[me] = meta_send[me]
 
     def scores_of(c):
-        g = c * QUAD // (HQ // KVH)
-        return dot(q[:, c * WIDE : (c + 1) * WIDE], keys[g], ((1,), (1,)))
+        g = c * QUAD // heads_per_key
+        four = q[:, c * WIDE : (c + 1) * WIDE]
+        none = jnp.zeros((), BF16)
+        stacked = jnp.concatenate(
+            [jnp.where(lane_head == i, four, none) for i in range(QUAD)], axis=0
+        )
+        return dot(stacked, keys[g], ((1,), (1,))) + bias
+
+    def by_pair(parts, lanes):
+        return jnp.concatenate(
+            [
+                jnp.where(
+                    lane < HD,
+                    parts[p * rows : (p + 1) * rows, lanes],
+                    parts[(p + 1) * rows : (p + 2) * rows, lanes],
+                )
+                for p in range(0, QUAD, 2)
+            ],
+            axis=1,
+        )
 
     def absorb(order, c):
         start = (base, far)[order]
@@ -277,22 +288,20 @@
     heads_per_key = HQ // KVH
     def attend(c, scores):
         lanes = slice(c * WIDE, (c + 1) * WIDE)
-        g = c * QUAD // heads_per_key
-        powers, carried, total = [], [], []
-        for i in range(QUAD):
-            part = scores[:, i * span : (i + 1) * span] + bias
-            head = c * QUAD + i
-            logs = logs_all[:, head : head + 1]
-            row_max = jnp.maximum(jnp.max(part, axis=1, keepdims=True), logs)
-            power = jnp.exp(part - row_max)
-            share = jnp.exp(logs - row_max)
-            carried.append(share)
-            total.append(share + jnp.sum(power, axis=1, keepdims=True))
-            powers.append(power.astype(BF16))
-        mixed = dot(jnp.concatenate(powers, axis=1), values[g])
+        logs = jnp.concatenate(
+            [logs_all[:, c * QUAD + i : c * QUAD + i + 1] for i in range(QUAD)], axis=0
+        )
+        row_max = jnp.maximum(jnp.max(scores, axis=1, keepdims=True), logs)
+        powers = jnp.exp(scores - row_max).astype(BF16)
+        carried = by_pair(
+            jnp.broadcast_to(jnp.exp(logs - row_max), (QUAD * rows, WIDE // 2)),
+            slice(0, WIDE // 2),
+        )
+        mixed = dot(powers, values[c * QUAD // heads_per_key])
+        total = carried + by_pair(mixed, slice(WIDE // 2, WIDE))
         result = (
-            spread(carried, rows) * prior[:, lanes].astype(F32) + mixed
-        ) / spread(total, rows)
+            carried * prior[:, lanes].astype(F32) + by_pair(mixed, slice(0, WIDE // 2))
+        ) / total
         result = result.astype(BF16)
         raw[c] = result
         raw_copy(c).start()
@@ -307,9 +316,6 @@
         if c < chunks:
             scores = ahead
             if c + 1 < chunks:
-                if (c + 1) * QUAD % heads_per_key == 0:
-                    for j in range(STEPS):
-                        lay_out((c + 1) * QUAD // heads_per_key, j)
                 ahead = scores_of(c + 1)
             attend(c, scores)
         if c == 0:
@@ -349,19 +355,22 @@
         out.wait()
 
 
-def hand_over(attended, hidden, attended_out, hidden_out, sems):
-    copies = []
-    for k, (source, target) in enumerate(((attended, attended_out), (hidden, hidden_out))):
+def hand_over(attended, hidden, attended_out, hidden_out, rows_held, hidden_held, sems):
+    fetches, stores = [], []
+    pairs = ((attended, rows_held, attended_out), (hidden, hidden_held, hidden_out))
+    for k, (source, held, target) in enumerate(pairs):
         step = source.shape[0] // PIECES
         for i in range(PIECES):
             part = pl.ds(i * step, step)
-            copies.append(
-                pltpu.make_async_copy(source.at[part], target.at[part], sems.at[k, i])
-            )
-    for one in copies:
-        one.start()
-    for one in copies:
-        one.wait()
+            fetches.append(pltpu.make_async_copy(source.at[part], held.at[part], sems.at[0, k, i]))
+            stores.append(pltpu.make_async_copy(held.at[part], target.at[part], sems.at[1, k, i]))
+    for fetch in fetches:
+        fetch.start()
+    for fetch, store in zip(fetches, stores):
+        fetch.wait()
+        store.start()
+    for store in stores:
+        store.wait()
 
 
 def per_device(
@@ -398,8 +407,8 @@
             pltpu.VMEM((IN_FLIGHT, rows), jnp.int32),
             pltpu.VMEM((IN_FLIGHT, rows), BF16),
             pltpu.VMEM((STEPS - 1, rows, pair_width), BF16),
-            pltpu.VMEM((KVH, QUAD * STEPS * rows, WIDE), BF16),
-            pltpu.VMEM((KVH, QUAD * STEPS * rows, WIDE), BF16),
+            pltpu.VMEM((KVH, STEPS * rows, WIDE), BF16),
+            pltpu.VMEM((KVH, STEPS * rows, WIDE), BF16),
             pltpu.VMEM((chunks, rows, WIDE), BF16),
             pltpu.VMEM((half_slots, rows), BF16),
             pltpu.VMEM((half_slots, rows), BF16),
@@ -443,7 +452,11 @@
         ),
         in_specs=[any_space] * 2,
         out_specs=(any_space, any_space),
-        scratch_shapes=[dma((2, PIECES))],
+        scratch_shapes=[
+            pltpu.VMEM((rows, width), BF16),
+            pltpu.VMEM((slots, hidden_width), BF16),
+            dma((2, 2, PIECES)),
+        ],
         compiler_params=pltpu.CompilerParams(vmem_limit_bytes=60 * 1024 * 1024),
     )(attended, hidden)
     hidden = hidden.reshape(exp_total, cap, hidden_width)[:, :capacity]

time: 80.2 us -> 46.9 us (0.58)
  Pallas kernels: 79.5 us -> 46.1 us
    pallas_call x1, Pallas kernels: 34.9 us -> 2.12 us  [per_device(): pl.pallas_call(hand_over, out_shape=(jax.ShapeDtypeStruct((rows, width),...]
where the time goes in v4:
time: 46.9 us; the launch traced here: 46.8 us
  Pallas kernels  46.1 us (98%)
  between operations  0.64 us (1%)
    pallas_call x1, Pallas kernels, per_device(): pl.pallas_call(functools.partial(kernel, ctx_total, exp_total, cap), out_...  44 us
    pallas_call x1, Pallas kernels, per_device(): pl.pallas_call(hand_over, out_shape=(jax.ShapeDtypeStruct((rows, width),...  2.12 us

profile of v4, /device:TPU:0, one launch (start us, length us, event | category | flops | bytes accessed | tf_op | source)
XLA Modules:
  0.0 46.8 jit_solution(15624345492962958790)
XLA Ops:
  0.6 44.0 %shard_map.104 = (bf16[128,2048]{1,0:T(8,128)(2,1)}, bf16[384,768]{1,0:T(8,128)(2,1)}) custom-call(bf16[128,2048]{1,0:T(8,128)(2,1)} %bitcast.19, bf16[128,256]{1,0:T(8,128)(2,1)} %bitcast.21, bf16[128,2048]{1,0:T(8,128)(2,1)} %bitcast.20, f32[32,128]{1,0:T(8,128)} %bitcast.22, f32[1,2048]{1,0:T(1,128)} %bitcast.23, bf16[2048,768]{1,0:T(8,128)(2,1)} %bitcast.17, ...), custom_call_target="tpu_custom_call" | custom-call | tf_op jit(solution)/shard_map/pallas_call | solution.py:391
  44.6 2.1 %shard_map.105 = (bf16[128,2048]{1,0:T(8,128)(2,1)}, bf16[384,768]{1,0:T(8,128)(2,1)}) custom-call(bf16[128,2048]{1,0:T(8,128)(2,1)} %get-tuple-element.6.attended, bf16[384,768]{1,0:T(8,128)(2,1)} %get-tuple-element.7.hidden), custom_call_target="tpu_custom_call" | custom-call | tf_op jit(solution)/shard_map/pallas_call | solution.py:447

commit v5 on v4

--- a/solution.py
+++ b/solution.py
@@ -18,6 +18,7 @@
 WIDE = 256
 QUAD = WIDE // HD
 PIECES = 4
+CORES = 2
 F32 = jnp.float32
 BF16 = jnp.bfloat16
 
@@ -53,7 +54,7 @@
 
 
 def kernel(
-    ctx_total, exp_total, cap,
+    ctx_total, exp_total, cap, share,
     query, key_value, prior_out, prior_lse, gain, w_gate, w_up, ids, weights,
     attended_out, hidden_out,
     q, kv, prior, lse, scale, wg, wu, id_rows, weight_rows,
@@ -72,7 +73,25 @@
     base = side * half
     local = me - base
     far = half - base
-    across = lax.rem(me + half, exp_total)
+    paired = share > 1
+    core = lax.rem(me, CORES)
+    if paired:
+        across = half + core - CORES * side
+        passes_on = me == half + core - CORES * (1 - side)
+        place = local // CORES
+        served = [far + core + CORES * k for k in range(share)]
+    else:
+        across = lax.rem(me + half, exp_total)
+        passes_on = None
+        place = 0
+        served = [across]
+
+    def if_passing(body):
+        if paired:
+            pl.when(passes_on)(body)
+        else:
+            body()
+
 
     loads = [
         pltpu.make_async_copy(a, b, local_sem.at[i])
@@ -125,8 +144,8 @@
     for one in passes:
         one.start()
     rank_copy = pltpu.make_async_remote_copy(
-        src_ref=rank_send, dst_ref=rank_recv, send_sem=rank_sems.at[0],
-        recv_sem=rank_sems.at[1], device_id={"exp": across}, device_id_type=MESH,
+        src_ref=rank_send, dst_ref=rank_recv.at[place], send_sem=rank_sems.at[share],
+        recv_sem=rank_sems.at[place], device_id={"exp": across}, device_id_type=MESH,
     )
     rank_copy.start()
     pick[...] = slot_rows(rank_send, base, half, cap, rows)
@@ -182,8 +201,8 @@
 
     def raw_copy(c):
         return pltpu.make_async_remote_copy(
-            src_ref=raw.at[c], dst_ref=relay_in.at[c], send_sem=raw_send.at[c],
-            recv_sem=raw_recv.at[c], device_id={"exp": across}, device_id_type=MESH,
+            src_ref=raw.at[c], dst_ref=relay_in.at[c, place], send_sem=raw_send.at[c],
+            recv_sem=raw_recv.at[c, place], device_id={"exp": across}, device_id_type=MESH,
         )
 
     def out_copy(c):
@@ -198,11 +217,31 @@
             device_id={"exp": to}, device_id_type=MESH,
         )
 
+    def relay_copy(c, k, to_local):
+        return pltpu.make_async_remote_copy(
+            src_ref=relay_out.at[c, k, slots_of(to_local)],
+            dst_ref=recv.at[c, slots_of(served[k])],
+            send_sem=relay_send.at[c, k, to_local], recv_sem=row_recv.at[c, served[k]],
+            device_id={"exp": base + to_local}, device_id_type=MESH,
+        )
+
     def pass_on(c):
-        raw_copy(c).wait_recv()
-        relay_out[c] = dot(relay_pick[...], relay_in[c]).astype(BF16)
-        each(1, half, lambda d: row_copy(c, peer(d), relay_out, relay_send, across).start())
-        recv[c, slots_of(across), :] = relay_out[c, slots_of(local), :]
+        for k in range(share):
+            pltpu.make_async_remote_copy(
+                src_ref=raw.at[c], dst_ref=relay_in.at[c, k], send_sem=raw_send.at[c],
+                recv_sem=raw_recv.at[c, k], device_id={"exp": across}, device_id_type=MESH,
+            ).wait_recv()
+            relay_out[c, k] = dot(relay_pick[k], relay_in[c, k]).astype(BF16)
+            each(1, half, lambda d, k=k: relay_copy(c, k, peer(d)).start())
+            recv[c, slots_of(served[k]), :] = relay_out[c, k, slots_of(local), :]
+
+    def ready():
+        for k in range(share):
+            pltpu.make_async_remote_copy(
+                src_ref=rank_send, dst_ref=rank_recv.at[k], send_sem=rank_sems.at[share],
+                recv_sem=rank_sems.at[k], device_id={"exp": across}, device_id_type=MESH,
+            ).wait_recv()
+            relay_pick[k] = slot_rows(rank_recv.at[k], base, half, cap, rows)
 
     diagonal = (iota((cap, rows), 0) == iota((cap, rows), 1)).astype(F32)
 
@@ -243,10 +282,19 @@
     def absorb(order, c):
         start = (base, far)[order]
         block_rows = pl.ds(pl.multiple_of(start * cap, cap), half * cap)
-        each(
-            1, half,
-            lambda d: row_copy(c, local, send, row_send, start + peer(d)).wait_recv(),
-        )
+        if order == 1 and paired:
+            for k in range(share):
+                row_copy(c, local, send, row_send, far + 1 - core + CORES * k).wait_recv()
+
+            @pl.when(jnp.logical_not(passes_on))
+            def _():
+                for k in range(share):
+                    row_copy(c, local, send, row_send, served[k]).wait_recv()
+        else:
+            each(
+                1, half,
+                lambda d: row_copy(c, local, send, row_send, start + peer(d)).wait_recv(),
+            )
         block = recv[c, block_rows, :].astype(F32)
         square = jnp.sum(block * block, axis=1, keepdims=True)
         lanes = slice(c * WIDE, (c + 1) * WIDE)
@@ -266,7 +314,7 @@
         start = (base, far)[order]
         each(1, half, lambda d: meta_copy(me, start + peer(d)).wait_recv())
         if order == 1:
-            meta_copy(me, across).wait_recv()
+            meta_copy(me, start + local).wait_recv()
         slot_weight = jnp.concatenate(
             [
                 jnp.sum(diagonal * meta_recv[start + s][:1, :], axis=1, keepdims=True)
@@ -319,12 +367,11 @@
                 ahead = scores_of(c + 1)
             attend(c, scores)
         if c == 0:
-            rank_copy.wait_recv()
-            relay_pick[...] = slot_rows(rank_recv, base, half, cap, rows)
+            if_passing(ready)
         if c == 1:
             send_weights()
         if 0 <= c - lag < chunks:
-            pass_on(c - lag)
+            if_passing(functools.partial(pass_on, c - lag))
         if c == near_lag:
             loads[6].wait()
             loads[7].wait()
@@ -348,9 +395,14 @@
     def sent(d):
         for c in range(chunks):
             row_copy(c, peer(d), send, row_send, me).wait_send()
-            row_copy(c, peer(d), relay_out, relay_send, across).wait_send()
+
+    def passed_on():
+        for c in range(chunks):
+            for k in range(share):
+                each(1, half, lambda d: relay_copy(c, k, peer(d)).wait_send())
 
     each(1, half, sent)
+    if_passing(passed_on)
     for out in stores:
         out.wait()
 
@@ -386,10 +438,11 @@
     pair_width = key_value.shape[2]
     any_space = pl.BlockSpec(memory_space=pl.ANY)
     dma = pltpu.SemaphoreType.DMA
+    share = 2 if exp_total == 4 * CORES else 1
     slots = exp_total * cap
     half_slots = exp_total // 2 * cap
     attended, hidden = pl.pallas_call(
-        functools.partial(kernel, ctx_total, exp_total, cap),
+        functools.partial(kernel, ctx_total, exp_total, cap, share),
         out_shape=(
             jax.ShapeDtypeStruct((rows, width), BF16),
             jax.ShapeDtypeStruct((slots, hidden_width), BF16),
@@ -411,13 +464,13 @@
             pltpu.VMEM((KVH, STEPS * rows, WIDE), BF16),
             pltpu.VMEM((chunks, rows, WIDE), BF16),
             pltpu.VMEM((half_slots, rows), BF16),
-            pltpu.VMEM((half_slots, rows), BF16),
+            pltpu.VMEM((share, half_slots, rows), BF16),
             pltpu.VMEM((chunks, half_slots, WIDE), BF16),
-            pltpu.VMEM((chunks, rows, WIDE), BF16),
-            pltpu.VMEM((chunks, half_slots, WIDE), BF16),
+            pltpu.VMEM((chunks, share, rows, WIDE), BF16),
+            pltpu.VMEM((chunks, share, half_slots, WIDE), BF16),
             pltpu.VMEM((chunks, slots, WIDE), BF16),
             pltpu.VMEM((exp_total, rows), F32),
-            pltpu.VMEM((exp_total, rows), F32),
+            pltpu.VMEM((share, exp_total, rows), F32),
             pltpu.VMEM((exp_total, 8, rows), F32),
             pltpu.VMEM((exp_total, 8, rows), F32),
             pltpu.VMEM((2, half_slots, 1), F32),
@@ -430,10 +483,10 @@
             dma((STEPS - 1,)),
             dma((chunks, exp_total // 2)),
             dma((chunks, exp_total)),
-            dma((chunks, exp_total // 2)),
+            dma((chunks, share, exp_total // 2)),
             dma((chunks,)),
-            dma((chunks,)),
-            dma((2,)),
+            dma((chunks, share)),
+            dma((share + 1,)),
             dma((exp_total,)),
             dma((exp_total,)),
         ],

time: 46.9 us -> 47.5 us (1.013)
  no operation moved by 1% of the time
where the time goes in v5:
time: 47.5 us; the launch traced here: 47.3 us
  Pallas kernels  46.5 us (98%)
  between operations  0.8 us (2%)
    pallas_call x1, Pallas kernels, per_device(): pl.pallas_call(functools.partial(kernel, ctx_total, exp_total, cap, share...  44.4 us
    pallas_call x1, Pallas kernels, per_device(): pl.pallas_call(hand_over, out_shape=(jax.ShapeDtypeStruct((rows, width),...  2.12 us

profile of v5, /device:TPU:0, one launch (start us, length us, event | category | flops | bytes accessed | tf_op | source)
XLA Modules:
  0.0 47.3 jit_solution(8041756111909792796)
XLA Ops:
  0.6 44.4 %shard_map.104 = (bf16[128,2048]{1,0:T(8,128)(2,1)}, bf16[384,768]{1,0:T(8,128)(2,1)}) custom-call(bf16[128,2048]{1,0:T(8,128)(2,1)} %bitcast.19, bf16[128,256]{1,0:T(8,128)(2,1)} %bitcast.21, bf16[128,2048]{1,0:T(8,128)(2,1)} %bitcast.20, f32[32,128]{1,0:T(8,128)} %bitcast.22, f32[1,2048]{1,0:T(1,128)} %bitcast.23, bf16[2048,768]{1,0:T(8,128)(2,1)} %bitcast.17, ...), custom_call_target="tpu_custom_call" | custom-call | tf_op jit(solution)/shard_map/pallas_call | solution.py:444
  45.0 2.1 %shard_map.105 = (bf16[128,2048]{1,0:T(8,128)(2,1)}, bf16[384,768]{1,0:T(8,128)(2,1)}) custom-call(bf16[128,2048]{1,0:T(8,128)(2,1)} %get-tuple-element.6.attended, bf16[384,768]{1,0:T(8,128)(2,1)} %get-tuple-element.7.hidden), custom_call_target="tpu_custom_call" | custom-call | tf_op jit(solution)/shard_map/pallas_call | solution.py:500

commit v6 on v5

--- a/solution.py
+++ b/solution.py
@@ -279,9 +279,7 @@
             axis=1,
         )
 
-    def absorb(order, c):
-        start = (base, far)[order]
-        block_rows = pl.ds(pl.multiple_of(start * cap, cap), half * cap)
+    def await_rows(order, c):
         if order == 1 and paired:
             for k in range(share):
                 row_copy(c, local, send, row_send, far + 1 - core + CORES * k).wait_recv()
@@ -291,17 +289,26 @@
                 for k in range(share):
                     row_copy(c, local, send, row_send, served[k]).wait_recv()
         else:
+            start = (base, far)[order]
             each(
                 1, half,
                 lambda d: row_copy(c, local, send, row_send, start + peer(d)).wait_recv(),
             )
-        block = recv[c, block_rows, :].astype(F32)
+
+    def absorb(order, pair):
+        start = (base, far)[order]
+        block_rows = pl.ds(pl.multiple_of(start * cap, cap), half * cap)
+        for c in (2 * pair, 2 * pair + 1):
+            await_rows(order, c)
+        block = jnp.concatenate(
+            [recv[c, block_rows, :].astype(F32) for c in (2 * pair, 2 * pair + 1)], axis=1
+        )
         square = jnp.sum(block * block, axis=1, keepdims=True)
-        lanes = slice(c * WIDE, (c + 1) * WIDE)
+        lanes = slice(2 * pair * WIDE, (2 * pair + 2) * WIDE)
         scaled = (block * scale[:, lanes]).astype(BF16)
         gate = dot(scaled, wg[lanes, :])
         up = dot(scaled, wu[lanes, :])
-        if c == 0:
+        if pair == 0:
             squares[order] = square
             gates[order] = gate
             ups[order] = up
@@ -358,7 +365,7 @@
         out_copy(c).start()
         recv[c, slots_of(me), :] = send[c, slots_of(local), :]
 
-    lag, near_lag, far_lag = 2, 3, 5
+    lag, near_lag, far_lag = 2, 5, 8
     ahead = scores_of(0)
     for c in range(chunks + far_lag):
         if c < chunks:
@@ -376,12 +383,12 @@
             loads[6].wait()
             loads[7].wait()
             loads[8].wait()
-        if 0 <= c - near_lag < chunks:
-            absorb(0, c - near_lag)
+        if 0 <= c - near_lag < chunks and (c - near_lag) % 2 == 0:
+            absorb(0, (c - near_lag) // 2)
         if c - near_lag == chunks - 1:
             stores = [finish(0)]
-        if 0 <= c - far_lag < chunks:
-            absorb(1, c - far_lag)
+        if 0 <= c - far_lag < chunks and (c - far_lag) % 2 == 0:
+            absorb(1, (c - far_lag) // 2)
     stores.append(finish(1))
 
     for one in passes:

time: 47.5 us -> 47.5 us (level)
  no operation moved by 1% of the time
where the time goes in v6:
time: 47.5 us; the launch traced here: 47.3 us
  Pallas kernels  46.7 us (98%)
  between operations  0.64 us (1%)
    pallas_call x1, Pallas kernels, per_device(): pl.pallas_call(functools.partial(kernel, ctx_total, exp_total, cap, share...  44.5 us
    pallas_call x1, Pallas kernels, per_device(): pl.pallas_call(hand_over, out_shape=(jax.ShapeDtypeStruct((rows, width),...  2.12 us

profile of v6, /device:TPU:0, one launch (start us, length us, event | category | flops | bytes accessed | tf_op | source)
XLA Modules:
  0.0 47.3 jit_solution(17580867591386803903)
XLA Ops:
  0.6 44.5 %shard_map.104 = (bf16[128,2048]{1,0:T(8,128)(2,1)}, bf16[384,768]{1,0:T(8,128)(2,1)}) custom-call(bf16[128,2048]{1,0:T(8,128)(2,1)} %bitcast.19, bf16[128,256]{1,0:T(8,128)(2,1)} %bitcast.21, bf16[128,2048]{1,0:T(8,128)(2,1)} %bitcast.20, f32[32,128]{1,0:T(8,128)} %bitcast.22, f32[1,2048]{1,0:T(1,128)} %bitcast.23, bf16[2048,768]{1,0:T(8,128)(2,1)} %bitcast.17, ...), custom_call_target="tpu_custom_call" | custom-call | tf_op jit(solution)/shard_map/pallas_call | solution.py:451
  45.2 2.1 %shard_map.105 = (bf16[128,2048]{1,0:T(8,128)(2,1)}, bf16[384,768]{1,0:T(8,128)(2,1)}) custom-call(bf16[128,2048]{1,0:T(8,128)(2,1)} %get-tuple-element.6.attended, bf16[384,768]{1,0:T(8,128)(2,1)} %get-tuple-element.7.hidden), custom_call_target="tpu_custom_call" | custom-call | tf_op jit(solution)/shard_map/pallas_call | solution.py:507
